TPU v7x, 32 devices: a whole 2x2x4 slice. The times are simulated.
32 devices in a mesh: batch: 4 (over y, x), seq: 8 (over z, core).
Axes of the slice: x: 2, y: 2, z: 4, core: 2. Of those that a mesh axis runs over, the one named last changes fastest.
Arguments:
- tokens: bfloat16 [4, 1024, 960], P('batch', 'seq'), may hold values from -6 to 6
- group_ids: int32 [4, 1024], P('batch', 'seq'), may hold values from 0 to 3, as said below
- first_gain: float32 [960], replicated, may hold values from 0.1 to 1.9
- query_weight: bfloat16 [960, 960], replicated, may hold values from -0.1875 to 0.1875
- key_weight: bfloat16 [960, 320], replicated, may hold values from -0.1875 to 0.1875
- value_weight: bfloat16 [960, 320], replicated, may hold values from -0.1875 to 0.1875
- out_weight: bfloat16 [960, 960], replicated, may hold values from -1.5 to 1.5
- second_gain: float32 [960], replicated, may hold values from 0.1 to 1.9
- gate_weight: bfloat16 [960, 2560], replicated, may hold values from -0.1875 to 0.1875
- up_weight: bfloat16 [960, 2560], replicated, may hold values from -0.1875 to 0.1875
- down_weight: bfloat16 [2560, 960], replicated, may hold values from -0.125 to 0.125
- cotangent: bfloat16 [4, 1024, 960], P('batch', 'seq'), may hold values from -6 to 6
Outputs:
- layer_output: bfloat16 [4, 1024, 960], P('batch', 'seq')
- grad_tokens: bfloat16 [4, 1024, 960], P('batch', 'seq')
- first_gain_grad: float32 [960], replicated
- query_weight_grad: float32 [960, 960], replicated
- key_weight_grad: float32 [960, 320], replicated
- value_weight_grad: float32 [960, 320], replicated
- out_weight_grad: float32 [960, 960], replicated
- second_gain_grad: float32 [960], replicated
- gate_weight_grad: float32 [960, 2560], replicated
- up_weight_grad: float32 [960, 2560], replicated
- down_weight_grad: float32 [2560, 960], replicated
Inputs may be any that keep to these rules, and one draw needn't show every extreme that they name: `group_ids`: 4 document groups; a token attends to earlier tokens of its own group.
All inputs are finite; a program needn't handle non-finite values.
Results may differ from a plain program's by a relative error of at most 0.025.
Values may be sent and summed in bfloat16 or wider, within the bound.
No kernel may reach another device: no remote copies, remote signals or barrier semaphores. Data moves between devices by JAX's collectives and lax.ppermute only.
A program may use at most 256 MiB of HBM per device.

v0:
```python
import math

import jax
import jax.numpy as jnp
from jax import lax
from jax.sharding import PartitionSpec as P

D = 960
HEADS = 15
KV_HEADS = 5
HD = 64


epsilon = 1e-05


def from_behind(block, axis, distance):
    devices = range(lax.axis_size(axis))
    route = [(i - distance, i) for i in devices if i - distance in devices]
    return lax.ppermute(block, axis, route)


def shifted(block, axis, distance):
    devices = range(lax.axis_size(axis))
    route = [((i - distance) % len(devices), i) for i in devices]
    return lax.ppermute(block, axis, route)


def norm_rows(values_in, gain_vec):
    return (
        values_in
        * lax.rsqrt(jnp.mean(values_in * values_in, axis=-1, keepdims=True) + epsilon)
        * gain_vec
    )


def angles(positions):
    freqs = 10000.0 ** (-jnp.arange(HD // 2).astype(jnp.float32) * 2.0 / HD)
    turned = positions.astype(jnp.float32)[:, None] * freqs[None, :]
    return (jnp.cos(turned), jnp.sin(turned))


def rotate(values_in, cosine_table, sine_table):
    head_count = values_in.shape[-1] // HD
    shaped = values_in.reshape(values_in.shape[0], head_count, HD)
    half_width = HD // 2
    former = shaped[..., :half_width]
    latter = shaped[..., half_width:]
    cosine_b = cosine_table[:, None, :]
    sine_b = sine_table[:, None, :]
    turned = jnp.concatenate(
        [former * cosine_b - latter * sine_b, latter * cosine_b + former * sine_b], axis=-1
    )
    return turned.reshape(values_in.shape)


def attend_inputs(
    inputs, first_gain, query_weight, key_weight, value_weight, cosine_table, sine_table
):
    normed = norm_rows(inputs, first_gain).astype(jnp.bfloat16)
    query = rotate(
        jnp.dot(normed, query_weight, preferred_element_type=jnp.float32), cosine_table, sine_table
    ).astype(jnp.bfloat16)
    keys = rotate(
        jnp.dot(normed, key_weight, preferred_element_type=jnp.float32), cosine_table, sine_table
    ).astype(jnp.bfloat16)
    values = jnp.dot(normed, value_weight, preferred_element_type=jnp.float32).astype(jnp.bfloat16)
    return (normed, query, jnp.concatenate([keys, values], axis=1))


def feed_inputs(middle, second_gain, gate_weight, up_weight):
    second = norm_rows(middle, second_gain).astype(jnp.bfloat16)
    gate = jnp.dot(second, gate_weight, preferred_element_type=jnp.float32)
    upward = jnp.dot(second, up_weight, preferred_element_type=jnp.float32)
    product = (jax.nn.silu(gate) * upward).astype(jnp.bfloat16)
    return (second, gate, upward, product)


def block_scores(query_heads, key_block, allowed):
    key_rows = key_block.shape[0]
    key_heads = key_block[:, : KV_HEADS * HD].reshape(key_rows, KV_HEADS, HD)
    scores = jnp.einsum(
        "qkgd,skd->kgqs", query_heads, key_heads, preferred_element_type=jnp.float32
    ) * HD ** (-0.5)
    return jnp.where(allowed, scores, -1e30)


def body(
    tokens,
    group_ids,
    first_gain,
    query_weight,
    key_weight,
    value_weight,
    out_weight,
    second_gain,
    gate_weight,
    up_weight,
    down_weight,
    cotangent,
):
    row_count = tokens.shape[1]
    kv_width = KV_HEADS * HD
    group_size = HEADS // KV_HEADS
    cycle_size = lax.axis_size("seq")
    seq_index = lax.axis_index("seq")
    start_row = seq_index * row_count
    last_row = start_row + row_count - 1
    positions = start_row + jnp.arange(row_count, dtype=jnp.int32)
    cosine_table, sine_table = angles(positions)
    every_group = lax.all_gather(group_ids, "seq", axis=1, tiled=True)[0]
    own_groups = group_ids[0]
    inputs = tokens[0].astype(jnp.float32)
    normed, query, keyvals = attend_inputs(
        inputs, first_gain, query_weight, key_weight, value_weight, cosine_table, sine_table
    )
    query_heads = query.reshape(row_count, KV_HEADS, group_size, HD)
    start_state = (
        jnp.full((KV_HEADS, group_size, row_count), -1e30, jnp.float32),
        jnp.zeros((KV_HEADS, group_size, row_count), jnp.float32),
        jnp.zeros((KV_HEADS, group_size, row_count, HD), jnp.float32),
    )
    key_piece = lax.all_gather(keyvals, "seq", axis=0, tiled=True)
    piece_rows = key_piece.shape[0]
    block_rows = math.gcd(piece_rows, row_count)

    def one_block(block_index, current):
        first_key = block_index * block_rows

        def one_work(state):
            running_max, running_sum, weighted = state
            key_block = lax.dynamic_slice_in_dim(key_piece, block_index * block_rows, block_rows, 0)
            key_groups = lax.dynamic_slice_in_dim(every_group, first_key, block_rows, 0)
            key_pos = first_key + jnp.arange(block_rows, dtype=jnp.int32)
            allowed = (own_groups[:, None] == key_groups[None, :]) & (
                key_pos[None, :] <= positions[:, None]
            )
            scores = block_scores(query_heads, key_block, allowed)
            new_max = jnp.maximum(running_max, jnp.max(scores, axis=-1))
            shrink = jnp.exp(running_max - new_max)
            weights = jnp.where(allowed, jnp.exp(scores - new_max[..., None]), 0.0)
            running_sum = running_sum * shrink + jnp.sum(weights, axis=-1)
            value_heads = key_block[:, kv_width:].reshape(block_rows, KV_HEADS, HD)
            weighted = weighted * shrink[..., None] + jnp.einsum(
                "kgqs,skd->kgqd",
                weights.astype(jnp.bfloat16),
                value_heads,
                preferred_element_type=jnp.float32,
            )
            return (new_max, running_sum, weighted)

        return lax.cond(first_key <= last_row, one_work, lambda state: state, current)

    running_max, running_sum, weighted = lax.fori_loop(
        0, piece_rows // block_rows, one_block, start_state
    )
    attended = weighted / running_sum[..., None]
    log_total = running_max + jnp.log(running_sum)
    attended_low = attended.transpose(2, 0, 1, 3).reshape(row_count, D).astype(jnp.bfloat16)
    middle = inputs + jnp.dot(attended_low, out_weight, preferred_element_type=jnp.float32)
    second, gate, upward, product = feed_inputs(middle, second_gain, gate_weight, up_weight)
    result = middle + jnp.dot(product, down_weight, preferred_element_type=jnp.float32)
    layer_output = result.astype(jnp.bfloat16)[None]
    inputs_again, middle_again = lax.optimization_barrier((inputs, middle))
    normed, query, keyvals = attend_inputs(
        inputs_again, first_gain, query_weight, key_weight, value_weight, cosine_table, sine_table
    )
    second, gate, upward, product = feed_inputs(middle_again, second_gain, gate_weight, up_weight)
    outer = cotangent[0]
    down_weight_grad = jnp.dot(product.T, outer, preferred_element_type=jnp.float32)
    grad_product = jnp.dot(outer, down_weight.T, preferred_element_type=jnp.float32)
    unused_value, pull_gate = jax.vjp(
        lambda gate_in, up_in: jax.nn.silu(gate_in) * up_in, gate, upward
    )
    grad_gate, grad_up = pull_gate(grad_product)
    grad_gate = grad_gate.astype(jnp.bfloat16)
    grad_up = grad_up.astype(jnp.bfloat16)
    gate_weight_grad = jnp.dot(second.T, grad_gate, preferred_element_type=jnp.float32)
    up_weight_grad = jnp.dot(second.T, grad_up, preferred_element_type=jnp.float32)
    grad_second = jnp.dot(grad_gate, gate_weight.T, preferred_element_type=jnp.float32) + jnp.dot(
        grad_up, up_weight.T, preferred_element_type=jnp.float32
    )
    unused_second, pull_second = jax.vjp(norm_rows, middle, second_gain)
    grad_mid_norm, second_gain_grad = pull_second(grad_second)
    grad_middle = outer.astype(jnp.float32) + grad_mid_norm
    grad_branch = grad_middle.astype(jnp.bfloat16)
    out_weight_grad = jnp.dot(attended_low.T, grad_branch, preferred_element_type=jnp.float32)
    grad_attended = jnp.dot(grad_branch, out_weight.T, preferred_element_type=jnp.float32).astype(
        jnp.bfloat16
    )
    grad_heads = grad_attended.reshape(row_count, KV_HEADS, group_size, HD)
    row_delta = jnp.sum(grad_heads.astype(jnp.float32).transpose(1, 2, 0, 3) * attended, axis=-1)
    own_key_heads = keyvals[:, :kv_width].reshape(row_count, KV_HEADS, HD)
    own_value_heads = keyvals[:, kv_width:].reshape(row_count, KV_HEADS, HD)

    def back_step(cycle_step, carried):
        bundle, grad_query_acc, grads_kv = carried
        owner = (seq_index + cycle_step) % cycle_size
        first_query = owner * row_count

        def back_work(state):
            grads_state, query_state = state
            query_rows, grad_rows, delta_rows, total_rows = bundle
            far_query = query_rows.astype(jnp.bfloat16).reshape(row_count, KV_HEADS, group_size, HD)
            far_grad = grad_rows.astype(jnp.bfloat16).reshape(row_count, KV_HEADS, group_size, HD)
            query_groups = lax.dynamic_slice_in_dim(every_group, first_query, row_count, 0)
            query_pos = first_query + jnp.arange(row_count, dtype=jnp.int32)
            allowed = (query_groups[:, None] == own_groups[None, :]) & (
                positions[None, :] <= query_pos[:, None]
            )
            scores = block_scores(far_query, keyvals, allowed)
            weights = jnp.where(allowed, jnp.exp(scores - total_rows[..., None]), 0.0)
            grad_values = jnp.einsum(
                "kgqs,qkgd->skd",
                weights.astype(jnp.bfloat16),
                far_grad,
                preferred_element_type=jnp.float32,
            )
            grad_weights = jnp.einsum(
                "qkgd,skd->kgqs", far_grad, own_value_heads, preferred_element_type=jnp.float32
            )
            grad_scores = (weights * (grad_weights - delta_rows[..., None])).astype(jnp.bfloat16)
            query_state = query_state + jnp.einsum(
                "kgqs,skd->kgqd", grad_scores, own_key_heads, preferred_element_type=jnp.float32
            ) * HD ** (-0.5)
            grad_keys = jnp.einsum(
                "kgqs,qkgd->skd", grad_scores, far_query, preferred_element_type=jnp.float32
            ) * HD ** (-0.5)
            grads_state = grads_state + jnp.concatenate(
                [grad_keys.reshape(row_count, kv_width), grad_values.reshape(row_count, kv_width)],
                axis=1,
            )
            return (grads_state, query_state)

        grads_kv, grad_query_acc = lax.cond(
            owner >= seq_index, back_work, lambda state: state, (grads_kv, grad_query_acc)
        )
        bundle = (
            from_behind(bundle[0].astype(jnp.bfloat16), "seq", -1).astype(jnp.float32),
            from_behind(bundle[1].astype(jnp.bfloat16), "seq", -1).astype(jnp.float32),
            from_behind(bundle[2].astype(jnp.bfloat16), "seq", -1).astype(jnp.float32),
            from_behind(bundle[3].astype(jnp.bfloat16), "seq", -1).astype(jnp.float32),
        )
        grad_query_acc = shifted(grad_query_acc.astype(jnp.bfloat16), "seq", -1).astype(
            grad_query_acc.dtype
        )
        return (bundle, grad_query_acc, grads_kv)

    start_bundle = (
        query.astype(jnp.float32),
        grad_attended.astype(jnp.float32),
        row_delta,
        log_total,
    )
    start_back = (
        start_bundle,
        jnp.zeros((KV_HEADS, group_size, row_count, HD), jnp.float32),
        jnp.zeros((row_count, 2 * kv_width), jnp.float32),
    )
    unused_bundle, grad_query_acc, grads_kv = lax.fori_loop(0, cycle_size, back_step, start_back)
    grad_query = rotate(
        grad_query_acc.transpose(2, 0, 1, 3).reshape(row_count, D), cosine_table, -sine_table
    ).astype(jnp.bfloat16)
    grad_keys = rotate(grads_kv[:, :kv_width], cosine_table, -sine_table).astype(jnp.bfloat16)
    grad_values = grads_kv[:, kv_width:].astype(jnp.bfloat16)
    query_weight_grad = jnp.dot(normed.T, grad_query, preferred_element_type=jnp.float32)
    key_weight_grad = jnp.dot(normed.T, grad_keys, preferred_element_type=jnp.float32)
    value_weight_grad = jnp.dot(normed.T, grad_values, preferred_element_type=jnp.float32)
    grad_normed = jnp.dot(grad_query, query_weight.T, preferred_element_type=jnp.float32)
    grad_normed = grad_normed + jnp.dot(grad_keys, key_weight.T, preferred_element_type=jnp.float32)
    grad_normed = grad_normed + jnp.dot(
        grad_values, value_weight.T, preferred_element_type=jnp.float32
    )
    unused_first, pull_first = jax.vjp(norm_rows, inputs, first_gain)
    grad_in_norm, first_gain_grad = pull_first(grad_normed)
    grad_tokens = (grad_middle + grad_in_norm).astype(jnp.bfloat16)[None]
    pieces = (
        first_gain_grad,
        query_weight_grad,
        key_weight_grad,
        value_weight_grad,
        out_weight_grad,
        second_gain_grad,
        gate_weight_grad,
        up_weight_grad,
        down_weight_grad,
    )
    packed = jnp.concatenate([item.reshape(-1) for item in pieces])
    used_length = packed.shape[0]
    padding = -used_length % lax.axis_size(("batch", "seq"))
    packed = jnp.pad(packed, (0, padding))
    shares = lax.psum_scatter(packed, ("batch", "seq"), scatter_dimension=0, tiled=True)
    summed = lax.all_gather(
        shares.astype(jnp.bfloat16), ("batch", "seq"), axis=0, tiled=True
    ).astype(shares.dtype)
    unpacked = []
    offset = 0
    for item in pieces:
        length = item.size
        unpacked.append(summed[offset : offset + length].reshape(item.shape))
        offset = offset + length
    return (
        layer_output,
        grad_tokens,
        unpacked[0],
        unpacked[1],
        unpacked[2],
        unpacked[3],
        unpacked[4],
        unpacked[5],
        unpacked[6],
        unpacked[7],
        unpacked[8],
    )


def solution(mesh):
    in_specs = (
        P("batch", "seq", None),
        P("batch", "seq"),
        P(),
        P(),
        P(),
        P(),
        P(),
        P(),
        P(),
        P(),
        P(),
        P("batch", "seq", None),
    )
    out_specs = (
        P("batch", "seq", None),
        P("batch", "seq", None),
        P(),
        P(),
        P(),
        P(),
        P(),
        P(),
        P(),
        P(),
        P(),
    )
    return jax.shard_map(body, mesh=mesh, in_specs=in_specs, out_specs=out_specs, check_vma=False)
```

profile of v0, /device:TPU:0, one launch (start us, length us, event | category | flops | bytes accessed | tf_op | source)
XLA Modules:
  0.0 1689.8 jit_solution(5848814329496864704)
XLA Ops:
  14.0 3.9 copy.43
  17.8 14.1 all_gather.9
  35.3 7.3 all-gather.2.cloned.1.call-done
  42.7 4.1 while.44
  42.9 3.5 conditional.6
  52.1 3.4 fusion.92
  65.2 157.5 %while.45 = (s32[]{:T(128)}, bf16[128,960]{0,1:T(8,128)(2,1)S(1)}, bf16[128,960]{0,1:T(8,128)(2,1)S(1)}, f32[5,3,128]{2,1,0:T(4,128)S(1)}, f32[5,3,128]{2,1,0:T(...) while((s32[]{:T(128)}, bf16[128,960]{0,1:T(8,128)(2,1)S(1)}, ...), condition=%wide.region_15.16_spmd.clone, body=%wide.region_12.15_spmd.clone.sunk | while | flops 160128784 | bytes 14794476 | solution.py:260
  65.3 5.2 conditional.7
  70.5 25.1 %collective-permute-start.4 = (bf16[5,3,128,64]{2,3,1,0:T(8,128)(2,1)S(1)}, bf16[5,3,128,64]{2,3,1,0:T(8,128)(2,1)S(1)}, u32[]{:S(2)}, u32[]{:S(2)}) collective-permute-start(bf16[5,3,128,64]{2,3,1,0:T(8,128)(2,1)S(1)} %convert_element_type.421), channel_id=1, source_target_pairs={{1,0},{2,1},{3,2},{4,3},{5,4},{6,5},{7,6},{0,7},{9,8},{10,9},{11,1... | collective-permute-start | bytes 737288 | tf_op jit(solution)/shard_map/while/body/eval_jaxpr/ppermute | solution.py:26
  105.3 5.2 conditional.7
  116.5 3.6 collective-permute-done.3
  122.3 5.2 conditional.7
  133.5 3.7 collective-permute-done.3
  139.3 5.2 conditional.7
  150.5 3.7 collective-permute-done.3
  156.4 5.2 conditional.7
  167.6 3.7 collective-permute-done.3
  173.4 5.2 conditional.7
  184.6 3.7 collective-permute-done.3
  190.5 5.2 conditional.7
  201.7 3.7 collective-permute-done.3
  207.6 5.2 conditional.7
  233.0 5.6 fusion.36
  238.6 5.3 fusion.99
  244.0 5.3 fusion.98
  249.3 2.9 reshape.349
  252.2 2.9 reshape.348
  255.1 5.5 reshape.350
  263.2 5.5 reshape.347
  268.7 13.1 reshape.353
  281.8 10.9 reshape.352
  292.7 11.1 reshape.351
  306.4 318.7 %concatenate.40 = f32[9832320]{0:T(1024)} concatenate(f32[960]{0:T(1024)S(1)} %get-tuple-element.752, f32[921600]{0:T(1024)} %reshape.347, f32[307200]{0:T(1024)} %reshape.348, f32[307200]{0:T(1024)} %reshape.349, f32[921600]{0:T(1024)} %reshape.350, f32[960]{0:T(1024)S(1)} %copy-done.39, f32[2457600]{0:T(1024)} %reshape.351, f32[2457600]{0:T(1024)} %reshape.352, f32[2457600]{0:T(1024)} %reshape.353), dimensions={0} | concatenate | bytes 78658560 | tf_op jit(solution)/shard_map/concatenate | solution.py:288
  625.1 638.3 %all-reduce.6 = bf16[9832320]{0:T(1024)(128)(2,1)} all-reduce(f32[9832320]{0:T(1024)} %concatenate.40), channel_id=2, replica_groups=mesh['batch'=4,'seq'=8] {'batch','seq'}, use_global_device_ids=true, to_apply=%region_19.20.clone | all-reduce | flops 9832320 | bytes 58993920
  1264.8 6.8 broadcast.203
  1271.6 10.2 dynamic-update-slice
  1283.7 3.3 fusion.53
  1287.0 7.2 fusion.35
  1294.2 302.4 %all-reduce.5.cloned.1.call-done = bf16[9832320]{0:T(1024)(128)(2,1)} async-done(((bf16[9832320]{0:T(1024)(128)(2,1)}), bf16[9832320]{0:T(1024)(128)(2,1)}) %all-reduce.5.cloned.1.call-update) | async-done | bytes 19664656
  1596.6 2.8 fusion.89
  1604.8 6.5 fusion.88
  1611.3 5.1 slice.148
  1616.4 5.1 slice.142
  1621.5 13.7 fusion.86
  1635.3 12.2 slice.153
  1647.5 11.2 copy.49
  1658.6 11.3 reshape.355
  1669.9 11.4 reshape.354
  (438 shorter events, 162.1 us)
Async XLA Ops:
  7.2 39.7 %copy-start = (bf16[960,960]{1,0:T(8,128)(2,1)S(1)}, bf16[960,960]{1,0:T(8,128)(2,1)}, u32[]{:S(2)}) copy-start(bf16[960,960]{1,0:T(8,128)(2,1)} %param.26) | copy-start | bytes 5529604
  7.2 35.4 %all-gather.2.cloned.1.call-start = ((), (), s32[]{:S(2)}) async-start(), calls=%async_computation | async-start | bytes 1474560 | tf_op jit(solution)/shard_map/all_gather | solution.py:123
  9.0 23.0 %copy-start.40 = (f32[128]{0:T(128)}, f32[128]{0:T(128)S(1)}, u32[]{:S(2)}) copy-start(f32[128]{0:T(128)S(1)} %fusion.80) | copy-start | bytes 1540
  13.1 21.3 %copy-start.31 = (f32[128,32]{0,1:T(8,128)}, f32[128,32]{0,1:T(8,128)S(1)}, u32[]{:S(2)}) copy-start(f32[128,32]{0,1:T(8,128)S(1)} %get-tuple-element.837) | copy-start | bytes 49156
  13.1 21.3 %copy-start.34 = (f32[128,32]{0,1:T(8,128)}, f32[128,32]{0,1:T(8,128)S(1)}, u32[]{:S(2)}) copy-start(f32[128,32]{0,1:T(8,128)S(1)} %get-tuple-element.836) | copy-start | bytes 49156
  13.9 1582.7 %all-reduce.5.cloned.1.call-start = ((), (), s32[]{:S(2)}) async-start(), calls=%async_computation.1 | async-start | bytes 39329792
  13.9 18.1 %copy-start.5 = (bf16[1,128,960]{1,2,0:T(8,128)(2,1)S(1)}, bf16[1,128,960]{1,2,0:T(8,128)(2,1)}, u32[]{:S(2)}) copy-start(bf16[1,128,960]{1,2,0:T(8,128)(2,1)} %param.20) | copy-start | bytes 737284
  13.9 18.1 %copy-start.37 = (f32[960]{0:T(1024)S(1)}, f32[960]{0:T(1024)}, u32[]{:S(2)}) copy-start(f32[960]{0:T(1024)} %param.22) | copy-start | bytes 11524
  70.5 34.6 %collective-permute-start.4 = (bf16[5,3,128,64]{2,3,1,0:T(8,128)(2,1)S(1)}, bf16[5,3,128,64]{2,3,1,0:T(8,128)(2,1)S(1)}, u32[]{:S(2)}, u32[]{:S(2)}) collective-permute-start(bf16[5,3,128,64]{2,3,1,0:T(8,128)(2,1)S(1)} %convert_element_type.421), channel_id=1, source_target_pairs={{1,0},{2,1},{3,2},{4,3},{5,4},{6,5},{7,6},{0,7},{9,8},{10,9},{11,1... | collective-permute-start | bytes 737288 | tf_op jit(solution)/shard_map/while/body/eval_jaxpr/ppermute | solution.py:26
  95.6 9.6 collective-permute-start
  96.9 8.3 collective-permute-start.1
  98.9 4.3 collective-permute-start.3
  100.2 4.9 collective-permute-start.2
  110.6 11.5 collective-permute-start.4
  110.6 11.5 collective-permute-start
  111.9 10.2 collective-permute-start.1
  113.9 6.2 collective-permute-start.3
  115.2 6.8 collective-permute-start.2
  127.5 11.6 collective-permute-start.4
  127.6 11.6 collective-permute-start
  128.9 10.3 collective-permute-start.1
  130.9 6.3 collective-permute-start.3
  132.2 6.9 collective-permute-start.2
  144.6 11.6 collective-permute-start.4
  144.6 11.6 collective-permute-start
  145.9 10.3 collective-permute-start.1
  147.9 6.3 collective-permute-start.3
  149.2 6.9 collective-permute-start.2
  161.6 11.6 collective-permute-start.4
  161.7 11.6 collective-permute-start
  163.0 10.3 collective-permute-start.1
  165.0 6.3 collective-permute-start.3
  166.3 6.9 collective-permute-start.2
  178.7 11.6 collective-permute-start.4
  178.7 11.6 collective-permute-start
  180.0 10.3 collective-permute-start.1
  182.0 6.3 collective-permute-start.3
  183.3 6.9 collective-permute-start.2
  195.7 11.6 collective-permute-start.4
  195.8 11.6 collective-permute-start
  197.1 10.3 collective-permute-start.1
  199.1 6.3 collective-permute-start.3
  200.4 6.9 collective-permute-start.2
  212.8 9.6 collective-permute-start.4
  212.8 9.6 collective-permute-start
  214.1 8.3 collective-permute-start.1
  216.1 4.3 collective-permute-start.3
  217.4 4.9 collective-permute-start.2
  (53 other events, 190.3 us)
Sparse Core Ops, SparseCore 0:
  14.0 28.5 all-gather.1
  1281.9 314.6 all-reduce.4
where the time goes:
time: 1720 us; the launch traced here: 1690 us
  blocking collectives  652 us (38%)
  local copies, waits for them, and re-layouts  491 us (29%)
  waiting for transfers between devices  346 us (20%)
  matrix products  89.9 us (5%)
  starting transfers between devices  66.8 us (4%)
  other arithmetic  26 us (2%)
    unnamed x1, blocking collectives  638 us
    concatenate x1, local copies, waits for them, and re-layouts, body(): packed = jnp.concatenate([item.reshape(-1) for item in pieces])  319 us
    unnamed x3, waiting for transfers between devices  302 us
    reshape x7, local copies, waits for them, and re-layouts, body(): packed = jnp.concatenate([item.reshape(-1) for item in pieces])  51.8 us
    slice x9, local copies, waits for them, and re-layouts, body(): unpacked.append(summed[offset:offset + length].reshape(item.shape))  49.2 us
    ppermute x32, starting transfers between devices, from_behind(): return lax.ppermute(block, axis, route)  41.2 us
    unnamed x109, local copies, waits for them, and re-layouts  40 us
    ppermute x32, waiting for transfers between devices, from_behind(): return lax.ppermute(block, axis, route)  36.2 us
  transfers between devices with their start and end apart: 42, of which 18 were waited for; matrix products, arithmetic and copies ran while one was open for 2% of the time, Pallas kernels for 0%

commit v1 on v0

v1 whole, which is shorter than its diff:
```python
import functools

import jax
import jax.numpy as jnp
import numpy as np
from jax import lax
from jax.experimental import pallas as pl
from jax.experimental.pallas import tpu as pltpu
from jax.sharding import Mesh
from jax.sharding import PartitionSpec as P

D = 960
HEADS = 15
KV_HEADS = 5
GROUP = HEADS // KV_HEADS
HD = 64
LANES = 128
WIDE = 1024
CHUNKS = WIDE // LANES
KVI = 2 * KV_HEADS * HD
QUARTER = 640
EXTRA = 16
EPS = 1e-05
MASKED = -1e30
F32 = jnp.float32
BF16 = jnp.bfloat16


def iota(shape, dim):
    return lax.broadcasted_iota(jnp.int32, shape, dim)


def dot(a, b):
    return lax.dot_general(a, b, (((1,), (0,)), ((), ())), preferred_element_type=F32)


def dot_rt(a, b):
    return lax.dot_general(a, b, (((1,), (1,)), ((), ())), preferred_element_type=F32)


def dot_lt(a, b):
    return lax.dot_general(a, b, (((0,), (0,)), ((), ())), preferred_element_type=F32)


def low_half(rows):
    return iota((rows, LANES), 1) < HD


def flip(v):
    return pltpu.roll(v, HD, 1)


def swap_halves(v):
    first = iota(v.shape, 1) % HD < HD // 2
    return jnp.where(first, pltpu.roll(v, LANES - HD // 2, 1), pltpu.roll(v, HD // 2, 1))


def whole(a):
    return pl.BlockSpec(a.shape, lambda *_, n=len(a.shape): (0,) * n)


ANY = pl.BlockSpec(memory_space=pl.ANY)


def call(kernel, out_shape, scalars, operands, scratch=(), grid=(1,), in_specs=None, out_specs=None, vmem=24, after=()):
    first, last = len(scalars) + len(operands), len(scalars) + len(operands) + len(after)

    def run(*refs):
        kernel(*refs[:first], *refs[last:])

    return pl.pallas_call(
        run,
        out_shape=out_shape,
        grid_spec=pltpu.PrefetchScalarGridSpec(
            num_scalar_prefetch=len(scalars),
            grid=grid,
            in_specs=(in_specs or [whole(a) for a in operands]) + [ANY] * len(after),
            out_specs=out_specs or [whole(a) for a in out_shape],
            scratch_shapes=list(scratch),
        ),
        compiler_params=pltpu.CompilerParams(vmem_limit_bytes=vmem * 1024 * 1024),
        cost_estimate=pl.CostEstimate(flops=1000, bytes_accessed=1000, transcendentals=0),
    )(*scalars, *operands, *after)


def shape(dims, dtype=BF16):
    return jax.ShapeDtypeStruct(tuple(dims), dtype)


def pre_kernel(info, tok, cot, grp, gain, freq, qw, kw, vw, x_o, pair_o, q_o, kv_o, groups_o, cos_o, sin_o, s1, s2):
    n = tok.shape[1]
    x = tok[...].astype(F32).T
    x_o[...] = x.astype(BF16)
    r = lax.rsqrt(jnp.mean(x * x, axis=-1, keepdims=True) + EPS)
    normed = (x * r * gain[...]).astype(BF16)
    pair_o[0] = normed
    pair_o[1] = cot[...].astype(F32).T.astype(BF16)
    groups = jnp.broadcast_to(grp[...].astype(F32), (n, n))
    groups_o[...] = groups.T
    turned = (info[0] + iota((n, LANES), 0)).astype(F32) * freq[...]
    cosine = jnp.cos(turned)
    sine = jnp.sin(turned)
    sine = jnp.where(iota((n, LANES), 1) % HD < HD // 2, -sine, sine)
    cos_o[...] = cosine
    sin_o[...] = sine
    low = low_half(n)
    kvw = KV_HEADS * HD
    s1[:, :kvw] = dot_rt(normed, kw[...])
    s2[:, :kvw] = dot_rt(normed, vw[...])
    for h in range(KV_HEADS):
        j = h // 2
        k = s1[:, j * LANES : (j + 1) * LANES]
        k = k * cosine + swap_halves(k) * sine
        v = s2[:, j * LANES : (j + 1) * LANES]
        both = jnp.where(low, flip(k), v) if h % 2 else jnp.where(low, k, flip(v))
        kv_o[0:n, h * LANES : (h + 1) * LANES] = both.astype(BF16)
    kv_o[n : n + EXTRA, 0:n] = groups[:EXTRA].astype(BF16)
    kv_o[n : n + EXTRA, n:] = jnp.zeros((EXTRA, KVI - n), BF16)
    s1[:, :D] = dot(normed, qw[...])
    for j in range(CHUNKS):
        v = s1[:, j * LANES : (j + 1) * LANES]
        v = v * cosine + swap_halves(v) * sine
        if (j + 1) * LANES > D:
            v = jnp.where(low, v, 0.0)
        q_o[:, j * LANES : (j + 1) * LANES] = v.astype(BF16)


def product_back_kernel(info, cot, dw, out):
    out[0] = dot(cot[0], dw[...])


def load_keys(info, groups, blocks, keys, bias):
    n = groups.shape[0]
    qpos = info[0] + iota((n, n), 0)
    for i, block in enumerate(blocks):
        core = info[2] if i % 2 == 0 else 1 - info[2]
        kpos = ((info[1] - i // 2) * 2 + core) * n + iota((n, n), 1)
        grow = block[n : n + EXTRA, 0:n].astype(F32)[0:1]
        allowed = (groups[...] == grow) & (kpos <= qpos) & (kpos >= 0)
        bias[:, i * n : (i + 1) * n] = jnp.where(allowed, 0.0, MASKED)
        keys[i * n : (i + 1) * n, :] = block[0:n, :]


def head_chunk(ref, head):
    return ref[:, head // 2 * LANES : (head // 2 + 1) * LANES].astype(F32)


def query_rows(q, h, low):
    rows = []
    for head in range(h * GROUP, (h + 1) * GROUP):
        v = head_chunk(q, head)
        v = flip(v) if head % 2 else v
        rows.append(jnp.where(low, v * HD**-0.5, 0.0).astype(BF16))
    return jnp.concatenate(rows, axis=0)


def attend_kernel(count, info, q, groups, *refs):
    blocks, (low_o, wide_o, lse_o, keys, bias) = refs[:count], refs[count:]
    n = groups.shape[0]
    low = low_half(n)
    load_keys(info, groups, blocks, keys, bias)
    lane = iota((n, LANES), 1)
    lse = jnp.zeros((n, LANES), F32)
    before = None
    for h in range(KV_HEADS):
        kv = keys[:, h * LANES : (h + 1) * LANES]
        scores = dot_rt(query_rows(q, h, low), kv)
        probs = []
        for g in range(GROUP):
            s = scores[g * n : (g + 1) * n] + bias[...]
            top = jnp.max(s, axis=-1, keepdims=True)
            e = jnp.exp(s - top)
            total = jnp.sum(e, axis=-1, keepdims=True)
            probs.append((e * (1.0 / total)).astype(BF16))
            lse = jnp.where(lane == h * GROUP + g, top + jnp.log(total), lse)
        mixed = dot(jnp.concatenate(probs, axis=0), kv)
        for g in range(GROUP):
            head = h * GROUP + g
            m = mixed[g * n : (g + 1) * n]
            j = head // 2
            if head % 2 == 0:
                before = flip(m)
                if head == HEADS - 1:
                    last = jnp.where(low, before, 0.0)
                    wide_o[:, j * LANES : (j + 1) * LANES] = last
                    low_o[:, j * LANES : D] = last[:, : D - j * LANES].astype(BF16)
            else:
                pair = jnp.where(low, before, m)
                wide_o[:, j * LANES : (j + 1) * LANES] = pair
                low_o[:, j * LANES : (j + 1) * LANES] = pair.astype(BF16)
    lse_o[...] = lse


def attend_back_kernel(count, info, q, groups, ga, wide, lse, cosine, sine, *refs):
    blocks = refs[:count]
    outs = refs[count:]
    gq_o, own_o, other_o, keys, bias = outs
    own_o[...] = jnp.zeros(own_o.shape, BF16)
    other_o[...] = jnp.zeros(other_o.shape, BF16)
    n = groups.shape[0]
    low = low_half(n)
    load_keys(info, groups, blocks, keys, bias)
    before = None
    for h in range(KV_HEADS):
        kv = keys[:, h * LANES : (h + 1) * LANES]
        rows = query_rows(q, h, low)
        scores = dot_rt(rows, kv)
        grads, deltas = [], []
        for head in range(h * GROUP, (h + 1) * GROUP):
            a = head_chunk(ga, head)
            w = head_chunk(wide, head)
            a = jnp.where(low, 0.0, a if head % 2 else flip(a))
            w = w if head % 2 else flip(w)
            deltas.append(jnp.sum(a * w, axis=-1, keepdims=True))
            grads.append(a.astype(BF16))
        grads = jnp.concatenate(grads, axis=0)
        grad_probs = dot_rt(grads, kv)
        probs, grad_scores = [], []
        for g in range(GROUP):
            head = h * GROUP + g
            p = jnp.exp(scores[g * n : (g + 1) * n] + bias[...] - lse[:, head : head + 1])
            probs.append(p.astype(BF16))
            grad_scores.append((p * (grad_probs[g * n : (g + 1) * n] - deltas[g])).astype(BF16))
        probs = jnp.concatenate(probs, axis=0)
        grad_scores = jnp.concatenate(grad_scores, axis=0)
        grad_kv = (dot_lt(grad_scores, rows) + dot_lt(probs, grads)).astype(BF16)
        for i in range(0, count, 2):

            @pl.when(info[1] >= i // 2)
            def _():
                for k, out in enumerate((own_o, other_o)):
                    out[info[1] - i // 2, :, h * LANES : (h + 1) * LANES] = grad_kv[(i + k) * n : (i + k + 1) * n]

        grad_q = dot(grad_scores, kv) * HD**-0.5
        for g in range(GROUP):
            head = h * GROUP + g
            m = grad_q[g * n : (g + 1) * n]
            j = head // 2
            if head % 2 == 0:
                before = m
                if head < HEADS - 1:
                    continue
                pair = jnp.where(low, m, 0.0)
            else:
                pair = jnp.where(low, before, flip(m))
            pair = pair * cosine[...] - swap_halves(pair) * sine[...]
            gq_o[:, j * LANES : (j + 1) * LANES] = pair.astype(BF16)


def norm_back(x, r, gain, grad):
    turned = grad * gain
    back = r * turned - x * (r * r * r) * jnp.mean(turned * x, axis=-1, keepdims=True)
    return back, jnp.sum(grad * x * r, axis=0, keepdims=True)


def feed_kernel(info, tok, att, cot, gain, ow, gp, gw, uw, dw, *refs):
    p_o, u_o, (out_o, gm_o, gb_o, ga_o, gg_o, middle, second, total, grad) = refs[:4], refs[4:8], refs[8:]
    step = pl.program_id(0)
    n = tok.shape[0]

    @pl.when(step == 0)
    def _():
        m = tok[...].astype(F32) + dot(att[...], ow[...])
        middle[...] = m
        r = lax.rsqrt(jnp.mean(m * m, axis=-1, keepdims=True) + EPS)
        second[...] = (m * r * gain[...]).astype(BF16)
        for u in u_o:
            u[:, 2 * QUARTER :] = second[...]
        total[...] = jnp.zeros((n, D), F32)
        grad[...] = jnp.zeros((n, D), F32)

    gate = dot(second[...], gw[...])
    up = dot(second[...], uw[...])
    sig = 1.0 / (1.0 + jnp.exp(-gate))
    silu = gate * sig
    product = (silu * up).astype(BF16)
    grad_product = gp[0]
    grad_gate = (grad_product * up * (sig * (1.0 + gate * (1.0 - sig)))).astype(BF16)
    grad_up = (grad_product * silu).astype(BF16)
    for k in range(4):

        @pl.when(step == k)
        def _():
            p_o[k][...] = product
            u_o[k][:, :QUARTER] = grad_gate
            u_o[k][:, QUARTER : 2 * QUARTER] = grad_up

    total[...] += dot_rt(product, dw[...])
    grad[...] += dot_rt(grad_gate, gw[...]) + dot_rt(grad_up, uw[...])

    @pl.when(step == pl.num_programs(0) - 1)
    def _():
        m = middle[...]
        out_o[...] = (m + total[...]).T.astype(BF16)
        r = lax.rsqrt(jnp.mean(m * m, axis=-1, keepdims=True) + EPS)
        back, gg_o[...] = norm_back(m, r, gain[...], grad[...])
        back = back + cot[0].astype(F32)
        gm_o[...] = back
        low = back.astype(BF16)
        zeros = jnp.zeros((n, WIDE - D), BF16)
        gb_o[:, :D] = low
        gb_o[:, D:] = zeros
        ga_o[:, :D] = dot_rt(low, ow[...]).astype(BF16)
        ga_o[:, D:] = zeros


def post_kernel(info, tok, gain, gm, gb, gq, gg2, att, cosine, sine, qw, kw, vw, mine, got, gt_o, *refs):
    pay_o, (packed, ks, vs) = refs[:4], refs[4:]
    n = tok.shape[0]
    low = low_half(n)
    heads = []
    for h in range(KV_HEADS):
        v = mine[0, :, h * LANES : (h + 1) * LANES].astype(F32) + got[0, :, h * LANES : (h + 1) * LANES].astype(F32)
        v = jnp.where(low, v * cosine[...] - swap_halves(v) * sine[...], v)
        packed[3, :, h * LANES : (h + 1) * LANES] = v.astype(BF16)
        heads.append(v)
    for j in range((KV_HEADS + 1) // 2):
        a = heads[2 * j]
        b = heads[2 * j + 1] if 2 * j + 1 < KV_HEADS else jnp.zeros_like(a)
        ks[:, j * LANES : (j + 1) * LANES] = jnp.where(low, a, flip(b)).astype(BF16)
        vs[:, j * LANES : (j + 1) * LANES] = jnp.where(low, flip(a), b).astype(BF16)
    kvw = KV_HEADS * HD
    grad = dot_rt(gq[:, :D], qw[...]) + dot(ks[:, :kvw], kw[...]) + dot(vs[:, :kvw], vw[...])
    x = tok[...].astype(F32)
    r = lax.rsqrt(jnp.mean(x * x, axis=-1, keepdims=True) + EPS)
    back, gain_grad = norm_back(x, r, gain[...], grad)
    gt_o[...] = (gm[...] + back).T.astype(BF16)
    for t in range(15):
        if t < 7:
            v = gq[:, t * LANES : (t + 1) * LANES]
        else:
            after = flip(gb[:, (t - 7) * LANES : (t - 6) * LANES].astype(F32))
            if t == 7:
                ahead = gq[:, 7 * LANES : 8 * LANES].astype(F32)
            else:
                ahead = flip(gb[:, (t - 8) * LANES : (t - 7) * LANES].astype(F32))
            v = jnp.where(low, ahead, after).astype(BF16)
        packed[t // 5, :, t % 5 * LANES : (t % 5 + 1) * LANES] = v
    row = iota((EXTRA, QUARTER), 0)
    rest = jnp.zeros((1, 2 * QUARTER - D), F32)
    gains = jnp.zeros((EXTRA, QUARTER), F32)
    for k, g in enumerate((gain_grad, gg2[...])):
        gains = jnp.where(row == 2 * k, g[:, :QUARTER], gains)
        gains = jnp.where(row == 2 * k + 1, jnp.concatenate([g[:, QUARTER:], rest], axis=1), gains)
    for k in range(4):
        pay_o[k][0:n, :QUARTER] = packed[k ^ info[3]]
        pay_o[k][n : n + EXTRA, :QUARTER] = gains.astype(BF16)
        pay_o[k][0:n, QUARTER:] = att[...]
        pay_o[k][n : n + EXTRA, QUARTER:] = jnp.zeros((EXTRA, D), BF16)


def split_store(info, total, send_o, keep_o):
    half, part = send_o.shape[0] * send_o.shape[1], send_o.shape[1]
    for k in range(2):
        there = pl.multiple_of((1 - info[2]) * half + k * part, 16)
        here = pl.multiple_of(info[2] * half + k * part, 16)
        send_o[k] = total[pl.ds(there, part), :].astype(BF16)
        keep_o[k] = total[pl.ds(here, part), :].astype(BF16)


def down_kernel(info, l0, l1, l2, l3, r0, r1, r2, r3, send_o, keep_o, left, right, total):
    n = r0.shape[0]
    for k, (a, b) in enumerate(zip((l0, l1, l2, l3), (r0, r1, r2, r3))):
        left[k * n : (k + 1) * n, :] = a[0]
        right[k * n : (k + 1) * n, :] = b[...]
    total[...] = dot_lt(left[...], right[...])
    split_store(info, total, send_o, keep_o)


def gate_kernel(info, u0, u1, u2, u3, send_o, keep_o, left, right, total):
    n = u0.shape[0]
    for k, u in enumerate((u0, u1, u2, u3)):
        left[k * n : (k + 1) * n, :] = u[:, 2 * QUARTER :]
        right[k * n : (k + 1) * n, :] = u[:, : 2 * QUARTER]
    total[...] = dot_lt(left[...], right[...])
    split_store(info, total, send_o, keep_o)


def mixed_kernel(info, n0, n1, n2, n3, p0, p1, p2, p3, send_o, keep_o, gains_o, left, right, total):
    n = n0.shape[1]
    column = info[3] * QUARTER + iota((n, QUARTER), 1)
    of_out = ((column >= D) & (column < 2 * D)).astype(F32)
    gains = jnp.zeros((EXTRA, QUARTER), F32)
    for k, (m, p) in enumerate(zip((n0, n1, n2, n3), (p0, p1, p2, p3))):
        left[k * n : (k + 1) * n, :] = m[0]
        left[(k + 4) * n : (k + 5) * n, :] = p[0:n, QUARTER:]
        g = p[0:n, :QUARTER].astype(F32)
        right[k * n : (k + 1) * n, :] = (g * (1.0 - of_out)).astype(BF16)
        right[(k + 4) * n : (k + 5) * n, :] = (g * of_out).astype(BF16)
        gains = gains + p[n : n + EXTRA, :QUARTER].astype(F32)
    gains_o[...] = gains.astype(BF16)
    total[...] = dot_lt(left[...], right[...])
    split_store(info, total, send_o, keep_o)


SLOTS = np.array([[0, 1], [2, 3], [4, 6], [5, 7], [8, 9], [10, 11], [12, 14], [13, 15]])


def widen_kernel(count, info, rows, columns, *refs):
    stacks, (*outs, raw, wide, came, went) = refs[:count], refs[count:]
    high, width = raw.shape[1], wide.shape[2] // len(outs)
    slots = wide.shape[0]
    pieces = [(i, k) for i in range(count) for k in range(stacks[i].shape[0])]

    def fetch(j):
        i, k = pieces[j]
        return pltpu.make_async_copy(stacks[i].at[k], raw.at[j], came.at[j])

    def store(j, k):
        place = outs[k].at[
            pl.ds(pl.multiple_of(rows[j] * high, 8), high), pl.ds(pl.multiple_of(columns[j] * width, LANES), width)
        ]
        return pltpu.make_async_copy(wide.at[j % slots, :, k * width : (k + 1) * width], place, went.at[j % slots, k])

    total = len(pieces)
    for j in range(total):
        fetch(j).start()
    for j in range(total):
        fetch(j).wait()
        for k in range(len(outs)):
            if j >= slots:
                store(j - slots, k).wait()
        wide[j % slots] = raw[j].astype(F32)
        for k in range(len(outs)):
            store(j, k).start()
    for j in range(total - slots, total):
        for k in range(len(outs)):
            store(j, k).wait()


def widen_attention_kernel(count, info, *refs):
    stacks, (q_o, k_o, v_o, o_o, raw, ks, vs, came) = refs[:count], refs[count:]
    step = pl.program_id(0)
    rows = raw.shape[1]
    low = low_half(rows)

    @pl.when(step == 0)
    def _():
        copies = []
        for i, stack in enumerate(stacks):
            for k in range(2):
                j = int(SLOTS[i, k])
                copies.append(pltpu.make_async_copy(stack.at[k], raw.at[j], came.at[j]))
        for copy in copies:
            copy.start()
        for copy in copies:
            copy.wait()

    base = ((step // 2) ^ info[2]) * 8 + ((step % 2) ^ (info[1] % 2)) * 4

    def chunk(t):
        return raw[base + ((t // 5) ^ info[3]), :, t % 5 * LANES : (t % 5 + 1) * LANES].astype(F32)

    for t in range(7):
        q_o[:, t * LANES : (t + 1) * LANES] = chunk(t)
    mixed = chunk(7)
    q_o[:, 7 * LANES : D] = mixed[:, : D - 7 * LANES]
    ahead = flip(mixed)
    for t in range(7):
        after = flip(chunk(8 + t))
        o_o[:, t * LANES : (t + 1) * LANES] = jnp.where(low, ahead, after)
        ahead = after
    o_o[:, 7 * LANES : D] = ahead[:, : D - 7 * LANES]
    place = pl.ds(pl.multiple_of(step * rows, 8), rows)
    for j in range(3):
        a = chunk(15 + 2 * j)
        b = chunk(16 + 2 * j) if j < 2 else jnp.zeros_like(a)
        ks[place, j * LANES : (j + 1) * LANES] = jnp.where(low, a, flip(b))
        vs[place, j * LANES : (j + 1) * LANES] = jnp.where(low, flip(a), b)

    @pl.when(step == pl.num_programs(0) - 1)
    def _():
        kvw = KV_HEADS * HD
        k_o[...] = ks[...].T[:kvw, :D]
        v_o[...] = vs[...].T[:kvw, :D]


def trade(v, axis, bit=0):
    size = lax.axis_size(axis)
    return lax.ppermute(v, axis, [(i, i ^ (1 << bit)) for i in range(size)])


def bits(axis, first=0):
    return range(first, lax.axis_size(axis).bit_length() - 1)


def sum_rest(v):
    for bit in bits("z", 1):
        v = v + trade(v, "z", bit)
    for bit in bits("far"):
        v = v + trade(v, "far", bit)
    return v


def halve_kernel(info, keep_away, got_away, keep_mine, got_mine, away_o, mine_o):
    away_o[...] = (keep_away[...].astype(F32) + got_away[...].astype(F32)).reshape(away_o.shape).astype(BF16)
    mine_o[...] = (keep_mine[...].astype(F32) + got_mine[...].astype(F32)).reshape(mine_o.shape).astype(BF16)


def stack_kernel(info, a, b, out):
    out[0] = a[...]
    out[1] = b[...]


class Line:
    def __init__(self, token):
        self.token = token

    def wait(self, *values):
        self.token, *values = lax.optimization_barrier((self.token, *values))
        return values

    def call(self, *args, token=0, **kwargs):
        outs = call(*args, after=[self.token], **kwargs)
        self.token = outs[token]
        return outs


def halve(line, info, bit, keep, got):
    count, _, high, width = keep.shape

    def part(away):
        return pl.BlockSpec((count, 1, high, width), lambda i, s: (0, ((s[1] >> bit) + away) % 2, 0, 0))

    return line.call(
        halve_kernel,
        [shape((count, high, width))] * 2,
        [info],
        [keep, got, keep, got],
        in_specs=[part(1), part(1), part(0), part(0)],
    )


class Chain:
    def __init__(self, line, info, pair):
        self.line, self.info = line, info
        self.send, self.keep = pair
        self.got = trade(self.send, "core")

    def halve(self):
        (got,) = self.line.wait(self.got)
        away, mine = halve(self.line, self.info, 0, self.keep[None], got[None])
        self.mine = mine[0]
        self.got = trade(away[0], "z")

    def total(self):
        mine, got = self.line.wait(self.mine, self.got)
        self.mine = mine + got
        (self.mine,) = self.line.wait(self.mine)
        steps = [("z", bit) for bit in bits("z", 1)] + [("far", bit) for bit in bits("far")]
        for axis, bit in steps[:-1]:
            self.mine = self.mine + trade(self.mine, axis, bit)
        self.got = trade(self.mine, *steps[-1])

    def spread(self):
        mine, got = self.line.wait(self.mine, self.got)
        (self.piece,) = self.line.wait(mine + got)
        self.over = trade(self.piece, "z")
        self.along_x = trade(self.piece, "x")

    def cross(self):
        (self.over,) = self.line.wait(self.over)
        self.along_y = trade(self.over, "y")

    def stack(self, a, b):
        return self.line.call(stack_kernel, [shape((2, *a.shape))], [self.info], [a, b])[0]

    def fill(self, which):
        if which == "y":
            (got,) = self.line.wait(self.along_x)
            self.first = self.stack(self.piece, got)
            self.first_y = trade(self.first, "y")
        else:
            (got,) = self.line.wait(self.along_y)
            self.second = self.stack(self.over, got)
            self.second_x = trade(self.second, "x")

    def share(self, which):
        if which == "own":
            self.others = [trade(self.first, "core"), None, trade(self.second, "core"), None]
        elif which == "y":
            (self.first_y,) = self.line.wait(self.first_y)
            self.others[1] = trade(self.first_y, "core")
        else:
            (self.second_x,) = self.line.wait(self.second_x)
            self.others[3] = trade(self.second_x, "core")

    def stacks(self):
        return self.line.wait(self.first, self.first_y, self.second, self.second_x, *self.others)


def to_plane(parts):
    far = lax.ppermute(parts[3], ("y", "x"), [(i, i ^ 3) for i in range(4)])
    return [parts[0], trade(parts[1], "x"), trade(parts[2], "y"), far]


def body(tokens, group_ids, first_gain, query_weight, key_weight, value_weight, out_weight, second_gain, gate_weight, up_weight, down_weight, cotangent):
    n = tokens.shape[1]
    z_size = lax.axis_size("z")
    z, core = lax.axis_index("z"), lax.axis_index("core")
    plane = lax.axis_index("y") * 2 + lax.axis_index("x")
    odd = z % 2
    info = jnp.stack([(z * 2 + core) * n, z, core, plane]).astype(jnp.int32)
    gain1, gain2 = first_gain[None], second_gain[None]
    freq = 10000.0 ** (-np.arange(HD // 2, dtype=np.float64) * 2.0 / HD)
    freq = jnp.asarray(np.tile(freq, LANES // (HD // 2))[None], F32)
    key_t, value_t, down_t = key_weight.T, value_weight.T, down_weight.T
    ff = gate_weight.shape[1]
    steps = ff // QUARTER
    square = shape((n, LANES), F32)

    x, pair, query, keyvals, groups, cosine, sine = call(
        pre_kernel,
        [shape((n, D)), shape((2, n, D)), shape((n, WIDE)), shape((n + EXTRA, KVI)), square, square, square],
        [info],
        [tokens[0].T, cotangent[0].T, group_ids, gain1, freq, query_weight, key_t, value_t],
        scratch=[pltpu.VMEM((n, WIDE), F32), pltpu.VMEM((n, 3 * LANES), F32)],
    )
    line = Line(cosine)
    blocks = [keyvals] + [
        lax.ppermute(keyvals, "z", [(i, i + distance) for i in range(z_size - distance)]) for distance in range(1, z_size)
    ]
    own_other = trade(keyvals, "core")
    pair_x = trade(pair, "x")
    cot_spec = pl.BlockSpec((1, n, D), lambda i, s: (1, 0, 0))
    quarter_spec = pl.BlockSpec((D, QUARTER), lambda i, s: (0, i ^ s[3]))
    (grad_product,) = line.call(
        product_back_kernel,
        [shape((steps, n, QUARTER), F32)],
        [info],
        [pair, down_t],
        grid=(steps,),
        in_specs=[cot_spec, quarter_spec],
        out_specs=[pl.BlockSpec((1, n, QUARTER), lambda i, s: (i, 0, 0))],
    )
    blocks = line.wait(*blocks)
    others = [own_other] + [trade(block, "core") for block in blocks[1:]]
    pair_y = trade(pair, "y")
    others = line.wait(*others)
    blocks = [b for both in zip(blocks, others) for b in both]

    keys = 2 * z_size * n
    attend_vmem = 16 + keys * 20 // 1024
    key_scratch = [pltpu.VMEM((keys, KVI), BF16), pltpu.VMEM((n, keys), F32)]
    attended, wide, lse = line.call(
        functools.partial(attend_kernel, len(blocks)),
        [shape((n, D)), shape((n, WIDE), F32), square],
        [info],
        [query, groups, *blocks],
        scratch=key_scratch,
        vmem=attend_vmem,
        token=2,
    )
    pair_x, pair_y = line.wait(pair_x, pair_y)
    (pair_now,) = line.wait(pair)
    pair_xy = lax.ppermute(pair_now, ("y", "x"), [(i, i ^ 3) for i in range(4)])

    feed_ins = [x, attended, pair, gain2, out_weight, grad_product, gate_weight, up_weight, down_t]
    feed_outs = (
        [shape((n, QUARTER))] * 4
        + [shape((n, 2 * QUARTER + D))] * 4
        + [shape((D, n)), shape((n, D), F32), shape((n, WIDE)), shape((n, WIDE)), shape((1, D), F32)]
    )
    *sides, result, grad_middle, grad_branch, grad_attended, gain2_part = line.call(
        feed_kernel,
        feed_outs,
        [info],
        feed_ins,
        scratch=[pltpu.VMEM((n, D), F32), pltpu.VMEM((n, D), BF16), pltpu.VMEM((n, D), F32), pltpu.VMEM((n, D), F32)],
        grid=(steps,),
        in_specs=[whole(x), whole(attended), cot_spec, whole(gain2), whole(out_weight)]
        + [pl.BlockSpec((1, n, QUARTER), lambda i, s: (i, 0, 0))]
        + [quarter_spec] * 3,
        token=12,
        vmem=28,
    )

    def weight_grad(kernel, operands, columns, specs=None, depth=4 * n, more=()):
        half = shape((2, D // 4, columns))
        return line.call(
            kernel,
            [half, half, *more],
            [info],
            operands,
            scratch=[pltpu.VMEM((depth, D), BF16), pltpu.VMEM((depth, columns), BF16), pltpu.VMEM((D, columns), F32)],
            in_specs=specs,
            vmem=28,
        )

    (pair_xy,) = line.wait(pair_xy)
    pairs = [pair, pair_x, pair_y, pair_xy]
    products, gate_ups = to_plane(sides[:4]), sides[4:]
    gate_x, gate_y = trade(gate_ups[1], "x"), trade(gate_ups[2], "y")
    grad_query, own, other = line.call(
        functools.partial(attend_back_kernel, len(blocks)),
        [shape((n, WIDE)), shape((z_size, n, KVI)), shape((z_size, n, KVI))],
        [info],
        [query, groups, grad_attended, wide, lse, cosine, sine, *blocks],
        scratch=key_scratch,
        vmem=attend_vmem + 4 + keys * 6 // 1024,
    )
    got = trade(other, "core")
    products = line.wait(*products)
    down = Chain(
        line, info, weight_grad(down_kernel, [*pairs, *products], QUARTER, [cot_spec] * 4 + [whole(p) for p in products])
    )
    own, got, gate_far = line.wait(own, got, gate_ups[3])
    gate_xy = lax.ppermute(gate_far, ("y", "x"), [(i, i ^ 3) for i in range(4)])
    for bit in bits("z"):
        if bit:
            own, got = line.wait(own, got)
        pairwise = (own.shape[0] // 2, 2, n, KVI)
        away, own = halve(line, info, bit, own.reshape(pairwise), got.reshape(pairwise))
        got = trade(away, "z", bit)
        if bit == 0:
            down.halve()
    down.total()
    gate_ups = line.wait(gate_ups[0], gate_x, gate_y, gate_xy)
    gate = Chain(line, info, weight_grad(gate_kernel, gate_ups, 2 * QUARTER))
    own, got = line.wait(own, got)
    kv3 = (KV_HEADS * HD + LANES - 1) // LANES * LANES
    grad_tokens, *payload = line.call(
        post_kernel,
        [shape((D, n))] + [shape((n + EXTRA, QUARTER + D))] * 4,
        [info],
        [x, gain1, grad_middle, grad_branch, grad_query, gain2_part, attended, cosine, sine, query_weight, key_t, value_t]
        + [own, got],
        scratch=[pltpu.VMEM((4, n, QUARTER), BF16), pltpu.VMEM((n, kv3), BF16), pltpu.VMEM((n, kv3), BF16)],
        token=1,
    )
    payloads = to_plane(payload)
    gate.halve()
    down.spread()
    down.cross()
    payloads = line.wait(*payloads)
    normed_spec = pl.BlockSpec((1, n, D), lambda i, s: (0, 0, 0))
    sa, ka, gains = weight_grad(
        mixed_kernel,
        [*pairs, *payloads],
        QUARTER,
        [normed_spec] * 4 + [whole(p) for p in payloads],
        8 * n,
        [shape((EXTRA, QUARTER))],
    )
    mixed = Chain(line, info, (sa, ka))
    gains_got = trade(gains, "core")
    down.fill("y")
    gate.total()
    mixed.halve()
    gains, gains_got = line.wait(gains, gains_got)
    gains = gains + gains_got
    gains_got = trade(gains, "z")
    down.fill("x")
    down.share("own")
    gains, gains_got = line.wait(gains, gains_got)
    gains = gains + gains_got
    mixed.total()
    down.share("y")
    down.share("x")

    slot = SLOTS.reshape(-1)
    block_row = ((core ^ (slot // 8)) * 2 + (odd ^ (slot // 4 % 2))).astype(jnp.int32)
    place = (plane ^ (slot % 4)).astype(jnp.int32)

    def widen(chain, count):
        stacks = chain.stacks()
        _, high, width = stacks[0].shape
        return line.call(
            functools.partial(widen_kernel, len(stacks)),
            [shape((D, ff), F32)] * count,
            [info, block_row, place],
            stacks,
            scratch=[
                pltpu.VMEM((16, high, width), BF16),
                pltpu.VMEM((4, high, width), F32),
                pltpu.SemaphoreType.DMA((16,)),
                pltpu.SemaphoreType.DMA((4, count)),
            ],
            in_specs=[ANY] * len(stacks),
            out_specs=[ANY] * count,
            vmem=24,
        )

    gate.spread()
    (down_grad,) = widen(down, 1)
    gate.cross()
    gate.fill("y")
    mixed.spread()
    gate.fill("x")
    gate.share("own")
    mixed.cross()
    gains = sum_rest(gains).astype(F32)
    gains = gains[:4].reshape(2, 2 * QUARTER)[:, :D]
    (gains,) = line.wait(gains)
    mixed.fill("y")
    gate.share("y")
    mixed.fill("x")
    mixed.share("own")
    gate.share("x")
    gate_grad, up_grad = widen(gate, 2)
    mixed.share("y")
    mixed.share("x")
    kvw = KV_HEADS * HD
    attention_outs = [shape((D, D), F32), shape((kvw, D), F32), shape((kvw, D), F32), shape((D, D), F32)]
    row_spec = pl.BlockSpec((D // 4, D), lambda i, s: (i, 0))
    stacks = mixed.stacks()
    query_grad, key_grad, value_grad, out_grad = line.call(
        functools.partial(widen_attention_kernel, len(stacks)),
        attention_outs,
        [info],
        stacks,
        grid=(4,),
        in_specs=[ANY] * len(stacks),
        out_specs=[row_spec, whole(attention_outs[1]), whole(attention_outs[2]), row_spec],
        scratch=[
            pltpu.VMEM((16, D // 4, QUARTER), BF16),
            pltpu.VMEM((WIDE, kv3), F32),
            pltpu.VMEM((WIDE, kv3), F32),
            pltpu.SemaphoreType.DMA((16,)),
        ],
        vmem=32,
    )
    return (
        result.T[None],
        grad_tokens.T[None],
        gains[0],
        query_grad,
        key_grad.T,
        value_grad.T,
        out_grad,
        gains[1],
        gate_grad,
        up_grad,
        down_grad.T,
    )


def solution(mesh):
    sizes = dict(mesh.shape)
    grid = Mesh(
        mesh.devices.reshape(sizes["batch"] // 4, 2, 2, sizes["seq"] // 2, 2),
        ("far", "y", "x", "z", "core"),
    )
    rows, columns = ("far", "y", "x"), ("z", "core")
    split = P(rows, columns, None)
    in_specs = (split, P(rows, columns)) + (P(),) * 9 + (split,)
    out_specs = (split, split) + (P(),) * 9
    return jax.shard_map(body, mesh=grid, in_specs=in_specs, out_specs=out_specs, check_vma=False)
```

time: 1720 us -> 320 us (0.19); the launches traced: 1690 us -> 318 us
  blocking collectives: 652 us -> 0 us
  local copies, waits for them, and re-layouts: 491 us -> 41.6 us
  waiting for transfers between devices: 346 us -> 141 us
  matrix products: 89.9 us -> 0 us
  Pallas kernels: 0 us -> 72.6 us
  other arithmetic: 26 us -> 1.46 us
    unnamed x1 -> x0, blocking collectives: 638 us -> none
    concatenate x1 -> x0, local copies, waits for them, and re-layouts: 319 us -> none  [body(): packed = jnp.concatenate([item.reshape(-1) for item in pieces])]
    unnamed x3 -> x0, waiting for transfers between devices: 302 us -> none
    ppermute x40 -> x61, waiting for transfers between devices: 36.2 us -> 141 us  [the longest x54 139 us: trade(): return lax.ppermute(v, axis, [(i, i ^ 1 << bit) for i in range(size)])]
    dot_general x67 -> x0, matrix products: 89.9 us -> none  [the longest x9 10.7 us: block_scores(): jnp.einsum('qkgd,skd->kgqs', query_heads, key_heads, preferred_element_ty...]
    reshape x9 -> x1, local copies, waits for them, and re-layouts: 74.5 us -> 0.02 us  [body(): gains = gains[:4].reshape(2, 2 * QUARTER)[:, :D]]
    pallas_call x0 -> x23, Pallas kernels: none -> 72.6 us  [call(): pl.pallas_call(run, out_shape=out_shape, grid_spec=pltpu.PrefetchScalarGr...]
    slice x11 -> x1, local copies, waits for them, and re-layouts: 50.2 us -> 0.6 us  [body(): gains[1]]
  transfers between devices with their start and end apart: 42 -> 61, of which waited for: 18 -> 27; matrix products, arithmetic and copies ran while one was open for 2% -> 3% of each run, Pallas kernels for 0% -> 16%
where the time goes in v1:
time: 320 us; the launch traced here: 318 us
  waiting for transfers between devices  141 us (44%)
  Pallas kernels  72.6 us (23%)
  starting transfers between devices  60.3 us (19%)
  local copies, waits for them, and re-layouts  41.6 us (13%)
    ppermute x54, waiting for transfers between devices, trade(): return lax.ppermute(v, axis, [(i, i ^ 1 << bit) for i in range(size)])  139 us
    pallas_call x23, Pallas kernels, call(): pl.pallas_call(run, out_shape=out_shape, grid_spec=pltpu.PrefetchScalarGr...  72.6 us
    ppermute x54, starting transfers between devices, trade(): return lax.ppermute(v, axis, [(i, i ^ 1 << bit) for i in range(size)])  42.5 us
    unnamed x98, local copies, waits for them, and re-layouts  29.8 us
    ppermute x3, starting transfers between devices, body(): lax.ppermute(keyvals, 'z', [(i, i + distance) for i in range(z_size - dis...  10.7 us
    optimization_barrier x4, local copies, waits for them, and re-layouts, wait(): self.token, *values = lax.optimization_barrier((self.token, *values))  6.92 us
  transfers between devices with their start and end apart: 61, of which 27 were waited for; matrix products, arithmetic and copies ran while one was open for 3% of the time, Pallas kernels for 16%

profile of v1, /device:TPU:0, one launch (start us, length us, event | category | flops | bytes accessed | tf_op | source)
XLA Modules:
  0.0 318.5 jit_solution(9915238519905892467)
XLA Ops:
  0.7 1.5 copy-done.4
  8.3 1.9 shard_map.239
  10.2 7.0 %collective-permute-start.2 = (bf16[144,640]{1,0:T(8,128)(2,1)S(1)}, bf16[144,640]{1,0:T(8,128)(2,1)S(1)}, u32[]{:S(2)}, u32[]{:S(2)}) collective-permute-start(bf16[144,640]{1,0:T(8,128)(2,1)S(1)} %get-tuple-element.214.refs_3_.refs_8_), channel_id=1, source_target_pairs={{0,6},{1,7},{8,14},{9,15},{16,22},{17,23},{24,30},{25,31}} | collective-permute-start | bytes 552968 | tf_op jit(solution)/shard_map/ppermute | solution.py:621
  17.2 1.6 collective-permute-start.8
  21.6 2.5 collective-permute-start
  24.1 2.4 copy-done.1
  26.5 2.6 shard_map.240.refs_11_.refs_6_
  31.4 4.6 %shard_map.241 = (bf16[128,960]{1,0:T(8,128)(2,1)S(1)}, f32[128,1024]{1,0:T(8,128)S(1)}, f32[128,128]{1,0:T(8,128)S(1)}) custom-call(s32[4]{0:T(128)S(1)} %pad_add_fusion.refs_0_, bf16[128,1024]{1,0:T(8,128)(2,1)S(1)} %get-tuple-element.209.refs_1_, f32[128,128]{1,0:T(8,128)S(1)} %get-tuple-element.210.refs_2_, ...), custom_call_target="tpu_custom_call" | custom-call | flops 1000 | bytes 1000 | tf_op jit(solution)/shard_map/pallas_call | solution.py:71
  36.0 2.1 collective-permute-start.9
  38.1 2.4 copy-done.6
  40.5 12.2 %shard_map.242 = (bf16[128,640]{1,0:T(8,128)(2,1)S(1)}, bf16[128,640]{1,0:T(8,128)(2,1)S(1)}, bf16[128,640]{1,0:T(8,128)(2,1)S(1)}, bf16[128,640]{1,0:T(8,128)(2...) custom-call(s32[4]{0:T(128)S(1)} %pad_add_fusion.refs_0_, ...), custom_call_target="tpu_custom_call" | custom-call | flops 1000 | bytes 1000 | tf_op jit(solution)/shard_map/pallas_call | solution.py:71
  54.8 9.1 %shard_map.243 = (bf16[128,1024]{1,0:T(8,128)(2,1)S(1)}, bf16[4,128,640]{2,1,0:T(8,128)(2,1)S(1)}, bf16[4,128,640]{2,1,0:T(8,128)(2,1)}) custom-call(s32[4]{0:T(128)S(1)} %pad_add_fusion.refs_0_, bf16[128,1024]{1,0:T(8,128)(2,1)S(1)} %get-tuple-element.209.refs_1_, f32[128,128]{1,0:T(8,128)S(1)} %get-tuple-element.210.refs_2_, ...), custom_call_target="tpu_custom_call" | custom-call | flops 1000 | bytes 1000 | tf_op jit(solution)/shard_map/pallas_call | solution.py:71
  65.5 2.0 collective-permute-start.12
  67.5 3.5 %collective-permute-done.10.refs_6_ = bf16[128,640]{1,0:T(8,128)(2,1)S(1)} collective-permute-done((bf16[128,640]{1,0:T(8,128)(2,1)S(1)}, bf16[128,640]{1,0:T(8,128)(2,1)S(1)}, u32[]{:S(2)}, u32[]{:S(2)}) %collective-permute-start.10) | collective-permute-done | bytes 163872 | tf_op jit(solution)/shard_map/ppermute | solution.py:480
  71.0 3.3 %collective-permute-done.11.refs_7_ = bf16[128,640]{1,0:T(8,128)(2,1)S(1)} collective-permute-done((bf16[128,640]{1,0:T(8,128)(2,1)S(1)}, bf16[128,640]{1,0:T(8,128)(2,1)S(1)}, u32[]{:S(2)}, u32[]{:S(2)}) %collective-permute-start.11) | collective-permute-done | bytes 163872 | tf_op jit(solution)/shard_map/ppermute | solution.py:480
  74.3 2.6 shard_map.244
  76.9 2.1 copy.27
  79.0 2.1 copy.28
  83.1 2.1 copy.29
  87.6 5.5 %collective-permute-start.15 = (bf16[2,128,640]{2,1,0:T(8,128)(2,1)S(1)}, bf16[2,128,640]{2,1,0:T(8,128)(2,1)S(1)}, u32[]{:S(2)}, u32[]{:S(2)}) collective-permute-start(bf16[2,128,640]{2,1,0:T(8,128)(2,1)S(1)} %get-tuple-element.260.refs_5_), channel_id=1, source_target_pairs={{0,2},{2,0},{4,6},{6,4},{1,3},{3,1},{5,7},{7,5},{8,10},{10,8},{12,... | collective-permute-start | bytes 983048 | tf_op jit(solution)/shard_map/ppermute | solution.py:480
  93.9 7.8 %collective-permute-done.15 = bf16[2,128,640]{2,1,0:T(8,128)(2,1)S(1)} collective-permute-done((bf16[2,128,640]{2,1,0:T(8,128)(2,1)S(1)}, bf16[2,128,640]{2,1,0:T(8,128)(2,1)S(1)}, u32[]{:S(2)}, u32[]{:S(2)}) %collective-permute-start.15) | collective-permute-done | bytes 327712 | tf_op jit(solution)/shard_map/ppermute | solution.py:480
  102.3 4.9 %collective-permute-done.16 = bf16[240,640]{1,0:T(8,128)(2,1)S(1)} collective-permute-done((bf16[240,640]{1,0:T(8,128)(2,1)S(1)}, bf16[240,640]{1,0:T(8,128)(2,1)S(1)}, u32[]{:S(2)}, u32[]{:S(2)}) %collective-permute-start.16) | collective-permute-done | bytes 307232 | tf_op jit(solution)/shard_map/ppermute | solution.py:480
  108.0 2.1 collective-permute-done.19
  113.6 2.2 copy.32.refs_4_
  118.9 2.3 shard_map.248
  121.2 7.5 %collective-permute-start.20 = (bf16[1,128,640]{2,1,0:T(8,128)(2,1)S(1)}, bf16[1,128,640]{2,1,0:T(8,128)(2,1)S(1)}, u32[]{:S(2)}, u32[]{:S(2)}) collective-permute-start(bf16[1,128,640]{2,1,0:T(8,128)(2,1)S(1)} %copy-done.36), channel_id=1, source_target_pairs={{0,4},{2,6},{4,0},{6,2},{1,5},{3,7},{5,1},{7,3},{8,12},{10,14},{12... | collective-permute-start | bytes 491528 | tf_op jit(solution)/shard_map/ppermute | solution.py:480
  128.8 15.0 %collective-permute-done.20.refs_14_ = bf16[1,128,640]{2,1,0:T(8,128)(2,1)S(1)} collective-permute-done((bf16[1,128,640]{2,1,0:T(8,128)(2,1)S(1)}, bf16[1,128,640]{2,1,0:T(8,128)(2,1)S(1)}, u32[]{:S(2)}, u32[]{:S(2)}) %collective-permute-start.20) | collective-permute-done | bytes 163872 | tf_op jit(solution)/shard_map/ppermute | solution.py:480
  147.7 2.8 shard_map.249
  150.5 1.5 collective-permute-start.24
  155.1 2.0 collective-permute-start.28
  157.1 8.2 %collective-permute-done.23.refs_1_ = bf16[240,640]{1,0:T(8,128)(2,1)S(1)} collective-permute-done((bf16[240,640]{1,0:T(8,128)(2,1)S(1)}, bf16[240,640]{1,0:T(8,128)(2,1)S(1)}, u32[]{:S(2)}, u32[]{:S(2)}) %collective-permute-start.23) | collective-permute-done | bytes 307232 | tf_op jit(solution)/shard_map/ppermute | solution.py:480
  165.3 9.2 %collective-permute-done.25.refs_7_ = bf16[144,1600]{1,0:T(8,128)(2,1)S(1)} collective-permute-done((bf16[144,1600]{1,0:T(8,128)(2,1)S(1)}, bf16[144,1600]{1,0:T(8,128)(2,1)S(1)}, u32[]{:S(2)}, u32[]{:S(2)}) %collective-permute-start.25) | collective-permute-done | bytes 460832 | tf_op jit(solution)/shard_map/ppermute | solution.py:480
  174.5 2.6 shard_map.251
  179.0 7.9 %collective-permute-done.27.refs_2_ = bf16[240,640]{1,0:T(8,128)(2,1)S(1)} collective-permute-done((bf16[240,640]{1,0:T(8,128)(2,1)S(1)}, bf16[240,640]{1,0:T(8,128)(2,1)S(1)}, u32[]{:S(2)}, u32[]{:S(2)}) %collective-permute-start.27) | collective-permute-done | bytes 307232 | tf_op jit(solution)/shard_map/ppermute | solution.py:480
  190.8 2.1 collective-permute-start.32
  192.9 19.8 %collective-permute-done.32 = bf16[16,640]{1,0:T(8,128)(2,1)S(1)} collective-permute-done((bf16[16,640]{1,0:T(8,128)(2,1)S(1)}, bf16[16,640]{1,0:T(8,128)(2,1)S(1)}, u32[]{:S(2)}, u32[]{:S(2)}) %collective-permute-start.32) | collective-permute-done | bytes 20512 | tf_op jit(solution)/shard_map/ppermute | solution.py:480
  217.5 5.8 %shard_map.255.refs_3_ = f32[960,2560]{1,0:T(8,128)} custom-call(s32[4]{0:T(128)S(1)} %pad_add_fusion.refs_0_, s32[16]{0:T(128)S(1)} %get-tuple-element.407.refs_1_, s32[16]{0:T(128)S(1)} %get-tuple-element.408.refs_2_, bf16[2,240,640]{2,1,0:T(8,128)(2,1)S(1)} %shard_map.252.refs_5_.refs_3_, bf16[2,240,640]{2,1,0:T(8,128)(2,1)S(1)} %collective-permute-done.34.refs_4_, ...), custom_call_target="tpu_custom_call" | custom-call | flops 1000 | bytes 1000 | tf_op jit(solution)/shard_map/pallas_call | solution.py:71
  223.3 6.8 %collective-permute-done.41.refs_1_ = bf16[240,1280]{1,0:T(8,128)(2,1)} collective-permute-done((bf16[240,1280]{1,0:T(8,128)(2,1)S(1)}, bf16[240,1280]{1,0:T(8,128)(2,1)}, u32[]{:S(2)}, u32[]{:S(2)}) %collective-permute-start.41) | collective-permute-done | bytes 614432 | tf_op jit(solution)/shard_map/ppermute | solution.py:480
  230.9 3.8 %copy-done = f32[960,2560]{1,0:T(8,128)S(1)} copy-done((f32[960,2560]{1,0:T(8,128)S(1)}, f32[960,2560]{1,0:T(8,128)}, u32[]{:S(2)}) %copy-start) | copy-done | bytes 9830424
  236.6 9.7 %collective-permute-done.43 = bf16[240,640]{1,0:T(8,128)(2,1)S(1)} collective-permute-done((bf16[240,640]{1,0:T(8,128)(2,1)S(1)}, bf16[240,640]{1,0:T(8,128)(2,1)S(1)}, u32[]{:S(2)}, u32[]{:S(2)}) %collective-permute-start.43) | collective-permute-done | bytes 307232 | tf_op jit(solution)/shard_map/ppermute | solution.py:480
  247.1 1.7 shard_map.257.refs_3_.refs_5_
  250.6 8.4 %collective-permute-done.45.refs_1_ = bf16[240,640]{1,0:T(8,128)(2,1)S(1)} collective-permute-done((bf16[240,640]{1,0:T(8,128)(2,1)S(1)}, bf16[240,640]{1,0:T(8,128)(2,1)S(1)}, u32[]{:S(2)}, u32[]{:S(2)}) %collective-permute-start.45) | collective-permute-done | bytes 307232 | tf_op jit(solution)/shard_map/ppermute | solution.py:480
  260.8 23.0 %collective-permute-done.47.refs_2_ = bf16[240,640]{1,0:T(8,128)(2,1)} collective-permute-done((bf16[240,640]{1,0:T(8,128)(2,1)S(1)}, bf16[240,640]{1,0:T(8,128)(2,1)}, u32[]{:S(2)}, u32[]{:S(2)}) %collective-permute-start.47) | collective-permute-done | bytes 307232 | tf_op jit(solution)/shard_map/ppermute | solution.py:480
  283.8 1.6 shard_map.258.refs_3_.refs_1_
  290.5 9.0 %shard_map.260 = (f32[960,2560]{1,0:T(8,128)}, f32[960,2560]{1,0:T(8,128)}) custom-call(s32[4]{0:T(128)S(1)} %pad_add_fusion.refs_0_, s32[16]{0:T(128)S(1)} %get-tuple-element.407.refs_1_, s32[16]{0:T(128)S(1)} %get-tuple-element.408.refs_2_, bf16[2,240,1280]{2,1,0:T(8,128)(2,1)S(1)} %shard_map.256.refs_3_, ...), custom_call_target="tpu_custom_call" | custom-call | flops 1000 | bytes 1000 | tf_op jit(solution)/shard_map/pallas_call | solution.py:71
  299.5 3.4 %collective-permute-done.55.refs_2_ = bf16[2,240,640]{2,1,0:T(8,128)(2,1)S(1)} collective-permute-done((bf16[2,240,640]{2,1,0:T(8,128)(2,1)S(1)}, bf16[2,240,640]{2,1,0:T(8,128)(2,1)S(1)}, u32[]{:S(2)}, u32[]{:S(2)}) %collective-permute-start.55) | collective-permute-done | bytes 614432 | tf_op jit(solution)/shard_map/ppermute | solution.py:480
  306.7 3.8 %copy-done.3 = f32[960,2560]{1,0:T(8,128)S(1)} copy-done((f32[960,2560]{1,0:T(8,128)S(1)}, f32[960,2560]{1,0:T(8,128)}, u32[]{:S(2)}) %copy-start.3) | copy-done | bytes 9830424
  310.5 7.7 %shard_map.261 = (f32[960,960]{1,0:T(8,128)}, f32[320,960]{1,0:T(8,128)}, f32[320,960]{1,0:T(8,128)}, f32[960,960]{1,0:T(8,128)}) custom-call(s32[4]{0:T(128)S(1)} %pad_add_fusion.refs_0_, bf16[2,240,640]{2,1,0:T(8,128)(2,1)S(1)} %shard_map.258.refs_3_.refs_1_, bf16[2,240,640]{2,1,0:T(8,128)(2,1)S(1)} %collective-permute-done.55.refs_2_, ...), custom_call_target="tpu_custom_call" | custom-call | flops 1000 | bytes 1000 | tf_op jit(solution)/shard_map/pallas_call | solution.py:71
  (215 shorter events, 61.6 us)
Async XLA Ops:
  10.2 13.8 %collective-permute-start.2 = (bf16[144,640]{1,0:T(8,128)(2,1)S(1)}, bf16[144,640]{1,0:T(8,128)(2,1)S(1)}, u32[]{:S(2)}, u32[]{:S(2)}) collective-permute-start(bf16[144,640]{1,0:T(8,128)(2,1)S(1)} %get-tuple-element.214.refs_3_.refs_8_), channel_id=1, source_target_pairs={{0,6},{1,7},{8,14},{9,15},{16,22},{17,23},{24,30},{25,31}} | collective-permute-start | bytes 552968 | tf_op jit(solution)/shard_map/ppermute | solution.py:621
  17.2 18.8 %collective-permute-start.8 = (bf16[2,128,960]{2,1,0:T(8,128)(2,1)S(1)}, bf16[2,128,960]{2,1,0:T(8,128)(2,1)S(1)}, u32[]{:S(2)}, u32[]{:S(2)}) collective-permute-start(bf16[2,128,960]{2,1,0:T(8,128)(2,1)S(1)} %get-tuple-element.235.refs_1_.refs_3_), channel_id=1, source_target_pairs={{0,16},{16,0},{1,17},{17,1},{2,18},{18,2},{3,19},{19,3},{4,20},{20... | collective-permute-start | bytes 1474568 | tf_op jit(solution)/shard_map/ppermute | solution.py:480
  18.8 17.3 %collective-permute-start.7 = (bf16[2,128,960]{2,1,0:T(8,128)(2,1)S(1)}, bf16[2,128,960]{2,1,0:T(8,128)(2,1)S(1)}, u32[]{:S(2)}, u32[]{:S(2)}) collective-permute-start(bf16[2,128,960]{2,1,0:T(8,128)(2,1)S(1)} %get-tuple-element.235.refs_1_.refs_3_), channel_id=1, source_target_pairs={{0,8},{8,0},{1,9},{9,1},{2,10},{10,2},{3,11},{11,3},{4,12},{12,4},... | collective-permute-start | bytes 1474568 | tf_op jit(solution)/shard_map/ppermute | solution.py:480
  20.3 8.9 %collective-permute-start.1 = (bf16[144,640]{1,0:T(8,128)(2,1)S(1)}, bf16[144,640]{1,0:T(8,128)(2,1)S(1)}, u32[]{:S(2)}, u32[]{:S(2)}) collective-permute-start(bf16[144,640]{1,0:T(8,128)(2,1)S(1)} %get-tuple-element.214.refs_3_.refs_8_), channel_id=1, source_target_pairs={{0,4},{2,6},{1,5},{3,7},{8,12},{10,14},{9,13},{11,15},{16,20},{18,... | collective-permute-start | bytes 552968 | tf_op jit(solution)/shard_map/ppermute | solution.py:621
  21.6 7.6 %collective-permute-start = (bf16[144,640]{1,0:T(8,128)(2,1)S(1)}, bf16[144,640]{1,0:T(8,128)(2,1)S(1)}, u32[]{:S(2)}, u32[]{:S(2)}) collective-permute-start(bf16[144,640]{1,0:T(8,128)(2,1)S(1)} %get-tuple-element.214.refs_3_.refs_8_), channel_id=1, source_target_pairs={{0,2},{2,4},{4,6},{1,3},{3,5},{5,7},{8,10},{10,12},{12,14},{9,11},... | collective-permute-start | bytes 552968 | tf_op jit(solution)/shard_map/ppermute | solution.py:621
  36.0 17.5 %collective-permute-start.9 = (bf16[2,128,960]{2,1,0:T(8,128)(2,1)S(1)}, bf16[2,128,960]{2,1,0:T(8,128)(2,1)S(1)}, u32[]{:S(2)}, u32[]{:S(2)}) collective-permute-start(bf16[2,128,960]{2,1,0:T(8,128)(2,1)S(1)} %get-tuple-element.235.refs_1_.refs_3_), channel_id=1, source_target_pairs={{0,24},{8,16},{16,8},{24,0},{1,25},{9,17},{17,9},{25,1},{2,26},{10... | collective-permute-start | bytes 1474568 | tf_op jit(solution)/shard_map/ppermute | solution.py:656
  63.9 19.2 %collective-permute-start.13 = (bf16[4,128,640]{2,1,0:T(8,128)(2,1)}, bf16[4,128,640]{2,1,0:T(8,128)(2,1)S(1)}, u32[]{:S(2)}, u32[]{:S(2)}) collective-permute-start(bf16[4,128,640]{2,1,0:T(8,128)(2,1)} %get-tuple-element.253), channel_id=1, source_target_pairs={{0,1},{1,0},{2,3},{3,2},{4,5},{5,4},{6,7},{7,6},{8,9},{9,8},{10,11... | collective-permute-start | bytes 1966088 | tf_op jit(solution)/shard_map/ppermute | solution.py:480
  63.9 7.1 %collective-permute-start.10 = (bf16[128,640]{1,0:T(8,128)(2,1)S(1)}, bf16[128,640]{1,0:T(8,128)(2,1)S(1)}, u32[]{:S(2)}, u32[]{:S(2)}) collective-permute-start(bf16[128,640]{1,0:T(8,128)(2,1)S(1)} %get-tuple-element.242), channel_id=1, source_target_pairs={{0,8},{8,0},{1,9},{9,1},{2,10},{10,2},{3,11},{11,3},{4,12},{12,4},... | collective-permute-start | bytes 491528 | tf_op jit(solution)/shard_map/ppermute | solution.py:480
  64.5 9.8 %collective-permute-start.11 = (bf16[128,640]{1,0:T(8,128)(2,1)S(1)}, bf16[128,640]{1,0:T(8,128)(2,1)S(1)}, u32[]{:S(2)}, u32[]{:S(2)}) collective-permute-start(bf16[128,640]{1,0:T(8,128)(2,1)S(1)} %get-tuple-element.243), channel_id=1, source_target_pairs={{0,16},{16,0},{1,17},{17,1},{2,18},{18,2},{3,19},{19,3},{4,20},{20... | collective-permute-start | bytes 491528 | tf_op jit(solution)/shard_map/ppermute | solution.py:480
  65.5 8.8 %collective-permute-start.12 = (bf16[128,640]{1,0:T(8,128)(2,1)S(1)}, bf16[128,640]{1,0:T(8,128)(2,1)S(1)}, u32[]{:S(2)}, u32[]{:S(2)}) collective-permute-start(bf16[128,640]{1,0:T(8,128)(2,1)S(1)} %get-tuple-element.244), channel_id=1, source_target_pairs={{0,24},{8,16},{16,8},{24,0},{1,25},{9,17},{17,9},{25,1},{2,26},{10... | collective-permute-start | bytes 491528 | tf_op jit(solution)/shard_map/ppermute | solution.py:593
  76.9 16.2 %collective-permute-start.14 = (bf16[2,240,640]{2,1,0:T(8,128)(2,1)}, bf16[2,240,640]{2,1,0:T(8,128)(2,1)S(1)}, u32[]{:S(2)}, u32[]{:S(2)}) collective-permute-start(bf16[2,240,640]{2,1,0:T(8,128)(2,1)} %get-tuple-element.257.refs_5_), channel_id=1, source_target_pairs={{0,1},{1,0},{2,3},{3,2},{4,5},{5,4},{6,7},{7,6},{8,9},{9,8},{10,11... | collective-permute-start | bytes 1843208 | tf_op jit(solution)/shard_map/ppermute | solution.py:480
  81.1 26.9 %collective-permute-start.18 = (bf16[128,2240]{0,1:T(8,128)(2,1)}, bf16[128,2240]{0,1:T(8,128)(2,1)}, u32[]{:S(2)}, u32[]{:S(2)}) collective-permute-start(bf16[128,2240]{0,1:T(8,128)(2,1)} %copy.28), channel_id=1, source_target_pairs={{0,16},{16,0},{1,17},{17,1},{2,18},{18,2},{3,19},{19,3},{4,20},{20... | collective-permute-start | bytes 1720328 | tf_op jit(solution)/shard_map/ppermute | solution.py:480
  82.3 25.7 %collective-permute-start.17 = (bf16[128,2240]{0,1:T(8,128)(2,1)}, bf16[128,2240]{0,1:T(8,128)(2,1)}, u32[]{:S(2)}, u32[]{:S(2)}) collective-permute-start(bf16[128,2240]{0,1:T(8,128)(2,1)} %copy.27), channel_id=1, source_target_pairs={{0,8},{8,0},{1,9},{9,1},{2,10},{10,2},{3,11},{11,3},{4,12},{12,4},... | collective-permute-start | bytes 1720328 | tf_op jit(solution)/shard_map/ppermute | solution.py:480
  85.2 25.0 %collective-permute-start.19 = (bf16[128,2240]{0,1:T(8,128)(2,1)}, bf16[128,2240]{0,1:T(8,128)(2,1)S(1)}, u32[]{:S(2)}, u32[]{:S(2)}) collective-permute-start(bf16[128,2240]{0,1:T(8,128)(2,1)} %copy.29), channel_id=1, source_target_pairs={{0,24},{8,16},{16,8},{24,0},{1,25},{9,17},{17,9},{25,1},{2,26},{10... | collective-permute-start | bytes 1720328 | tf_op jit(solution)/shard_map/ppermute | solution.py:708
  87.6 14.0 %collective-permute-start.15 = (bf16[2,128,640]{2,1,0:T(8,128)(2,1)S(1)}, bf16[2,128,640]{2,1,0:T(8,128)(2,1)S(1)}, u32[]{:S(2)}, u32[]{:S(2)}) collective-permute-start(bf16[2,128,640]{2,1,0:T(8,128)(2,1)S(1)} %get-tuple-element.260.refs_5_), channel_id=1, source_target_pairs={{0,2},{2,0},{4,6},{6,4},{1,3},{3,1},{5,7},{7,5},{8,10},{10,8},{12,... | collective-permute-start | bytes 983048 | tf_op jit(solution)/shard_map/ppermute | solution.py:480
  93.8 13.4 %collective-permute-start.16 = (bf16[240,640]{1,0:T(8,128)(2,1)S(1)}, bf16[240,640]{1,0:T(8,128)(2,1)S(1)}, u32[]{:S(2)}, u32[]{:S(2)}) collective-permute-start(bf16[240,640]{1,0:T(8,128)(2,1)S(1)} %bitcast.74), channel_id=1, source_target_pairs={{0,2},{2,0},{4,6},{6,4},{1,3},{3,1},{5,7},{7,5},{8,10},{10,8},{12,... | collective-permute-start | bytes 921608 | tf_op jit(solution)/shard_map/ppermute | solution.py:480
  121.2 32.8 %collective-permute-start.21 = (bf16[2,240,1280]{2,1,0:T(8,128)(2,1)S(1)}, bf16[2,240,1280]{2,1,0:T(8,128)(2,1)S(1)}, u32[]{:S(2)}, u32[]{:S(2)}) collective-permute-start(bf16[2,240,1280]{2,1,0:T(8,128)(2,1)S(1)} %get-tuple-element.285.refs_15_), channel_id=1, source_target_pairs={{0,1},{1,0},{2,3},{3,2},{4,5},{5,4},{6,7},{7,6},{8,9},{9,8},{10,11... | collective-permute-start | bytes 3686408 | tf_op jit(solution)/shard_map/ppermute | solution.py:480
  121.2 22.6 %collective-permute-start.20 = (bf16[1,128,640]{2,1,0:T(8,128)(2,1)S(1)}, bf16[1,128,640]{2,1,0:T(8,128)(2,1)S(1)}, u32[]{:S(2)}, u32[]{:S(2)}) collective-permute-start(bf16[1,128,640]{2,1,0:T(8,128)(2,1)S(1)} %copy-done.36), channel_id=1, source_target_pairs={{0,4},{2,6},{4,0},{6,2},{1,5},{3,7},{5,1},{7,3},{8,12},{10,14},{12... | collective-permute-start | bytes 491528 | tf_op jit(solution)/shard_map/ppermute | solution.py:480
  128.7 26.2 %collective-permute-start.22 = (bf16[240,640]{1,0:T(8,128)(2,1)}, bf16[240,640]{1,0:T(8,128)(2,1)S(1)}, u32[]{:S(2)}, u32[]{:S(2)}) collective-permute-start(bf16[240,640]{1,0:T(8,128)(2,1)} %add.42), channel_id=1, source_target_pairs={{0,4},{2,6},{4,0},{6,2},{1,5},{3,7},{5,1},{7,3},{8,12},{10,14},{12... | collective-permute-start | bytes 921608 | tf_op jit(solution)/shard_map/ppermute | solution.py:480
  150.5 14.8 %collective-permute-start.24 = (bf16[144,1600]{1,0:T(8,128)(2,1)S(1)}, bf16[144,1600]{1,0:T(8,128)(2,1)S(1)}, u32[]{:S(2)}, u32[]{:S(2)}) collective-permute-start(bf16[144,1600]{1,0:T(8,128)(2,1)S(1)} %get-tuple-element.300), channel_id=1, source_target_pairs={{0,8},{8,0},{1,9},{9,1},{2,10},{10,2},{3,11},{11,3},{4,12},{12,4},... | collective-permute-start | bytes 1382408 | tf_op jit(solution)/shard_map/ppermute | solution.py:480
  152.0 22.5 %collective-permute-start.25 = (bf16[144,1600]{1,0:T(8,128)(2,1)S(1)}, bf16[144,1600]{1,0:T(8,128)(2,1)S(1)}, u32[]{:S(2)}, u32[]{:S(2)}) collective-permute-start(bf16[144,1600]{1,0:T(8,128)(2,1)S(1)} %get-tuple-element.301), channel_id=1, source_target_pairs={{0,16},{16,0},{1,17},{17,1},{2,18},{18,2},{3,19},{19,3},{4,20},{20... | collective-permute-start | bytes 1382408 | tf_op jit(solution)/shard_map/ppermute | solution.py:480
  152.5 22.0 %collective-permute-start.26 = (bf16[144,1600]{1,0:T(8,128)(2,1)S(1)}, bf16[144,1600]{1,0:T(8,128)(2,1)S(1)}, u32[]{:S(2)}, u32[]{:S(2)}) collective-permute-start(bf16[144,1600]{1,0:T(8,128)(2,1)S(1)} %get-tuple-element.302), channel_id=1, source_target_pairs={{0,24},{8,16},{16,8},{24,0},{1,25},{9,17},{17,9},{25,1},{2,26},{10... | collective-permute-start | bytes 1382408 | tf_op jit(solution)/shard_map/ppermute | solution.py:593
  155.1 10.3 %collective-permute-start.23 = (bf16[240,640]{1,0:T(8,128)(2,1)S(1)}, bf16[240,640]{1,0:T(8,128)(2,1)S(1)}, u32[]{:S(2)}, u32[]{:S(2)}) collective-permute-start(bf16[240,640]{1,0:T(8,128)(2,1)S(1)} %add.45.refs_1_), channel_id=1, source_target_pairs={{0,2},{2,0},{4,6},{6,4},{1,3},{3,1},{5,7},{7,5},{8,10},{10,8},{12,... | collective-permute-start | bytes 921608 | tf_op jit(solution)/shard_map/ppermute | solution.py:480
  155.1 32.9 %collective-permute-start.28 = (bf16[240,1280]{1,0:T(8,128)(2,1)S(1)}, bf16[240,1280]{1,0:T(8,128)(2,1)S(1)}, u32[]{:S(2)}, u32[]{:S(2)}) collective-permute-start(bf16[240,1280]{1,0:T(8,128)(2,1)S(1)} %bitcast.70), channel_id=1, source_target_pairs={{0,2},{2,0},{4,6},{6,4},{1,3},{3,1},{5,7},{7,5},{8,10},{10,8},{12,... | collective-permute-start | bytes 1843208 | tf_op jit(solution)/shard_map/ppermute | solution.py:480
  177.1 11.1 %collective-permute-start.29 = (bf16[2,240,640]{2,1,0:T(8,128)(2,1)S(1)}, bf16[2,240,640]{2,1,0:T(8,128)(2,1)S(1)}, u32[]{:S(2)}, u32[]{:S(2)}) collective-permute-start(bf16[2,240,640]{2,1,0:T(8,128)(2,1)S(1)} %get-tuple-element.311.refs_3_), channel_id=1, source_target_pairs={{0,1},{1,0},{2,3},{3,2},{4,5},{5,4},{6,7},{7,6},{8,9},{9,8},{10,11... | collective-permute-start | bytes 1843208 | tf_op jit(solution)/shard_map/ppermute | solution.py:480
  177.2 9.7 %collective-permute-start.27 = (bf16[240,640]{1,0:T(8,128)(2,1)S(1)}, bf16[240,640]{1,0:T(8,128)(2,1)S(1)}, u32[]{:S(2)}, u32[]{:S(2)}) collective-permute-start(bf16[240,640]{1,0:T(8,128)(2,1)S(1)} %add.45.refs_1_), channel_id=1, source_target_pairs={{0,8},{8,0},{1,9},{9,1},{2,10},{10,2},{3,11},{11,3},{4,12},{12,4},... | collective-permute-start | bytes 921608 | tf_op jit(solution)/shard_map/ppermute | solution.py:480
  177.8 11.1 %collective-permute-start.31 = (bf16[240,640]{1,0:T(8,128)(2,1)S(1)}, bf16[240,640]{1,0:T(8,128)(2,1)S(1)}, u32[]{:S(2)}, u32[]{:S(2)}) collective-permute-start(bf16[240,640]{1,0:T(8,128)(2,1)S(1)} %collective-permute-done.23.refs_1_), channel_id=1, source_target_pairs={{0,16},{16,0},{1,17},{17,1},{2,18},{18,2},{3,19},{19,3},{4,20},{20... | collective-permute-start | bytes 921608 | tf_op jit(solution)/shard_map/ppermute | solution.py:480
  179.0 9.9 %collective-permute-start.30 = (bf16[16,640]{1,0:T(8,128)(2,1)S(1)}, bf16[16,640]{1,0:T(8,128)(2,1)S(1)}, u32[]{:S(2)}, u32[]{:S(2)}) collective-permute-start(bf16[16,640]{1,0:T(8,128)(2,1)S(1)} %get-tuple-element.324), channel_id=1, source_target_pairs={{0,1},{1,0},{2,3},{3,2},{4,5},{5,4},{6,7},{7,6},{8,9},{9,8},{10,11... | collective-permute-start | bytes 61448 | tf_op jit(solution)/shard_map/ppermute | solution.py:480
  187.5 25.9 %collective-permute-start.34 = (bf16[2,240,640]{2,1,0:T(8,128)(2,1)S(1)}, bf16[2,240,640]{2,1,0:T(8,128)(2,1)S(1)}, u32[]{:S(2)}, u32[]{:S(2)}) collective-permute-start(bf16[2,240,640]{2,1,0:T(8,128)(2,1)S(1)} %shard_map.252.refs_5_.refs_3_), channel_id=1, source_target_pairs={{0,16},{16,0},{1,17},{17,1},{2,18},{18,2},{3,19},{19,3},{4,20},{20... | collective-permute-start | bytes 1843208 | tf_op jit(solution)/shard_map/ppermute | solution.py:480
  189.5 23.9 %collective-permute-start.35 = (bf16[2,240,640]{2,1,0:T(8,128)(2,1)S(1)}, bf16[2,240,640]{2,1,0:T(8,128)(2,1)S(1)}, u32[]{:S(2)}, u32[]{:S(2)}) collective-permute-start(bf16[2,240,640]{2,1,0:T(8,128)(2,1)S(1)} %shard_map.254.refs_5_.refs_11_), channel_id=1, source_target_pairs={{0,8},{8,0},{1,9},{9,1},{2,10},{10,2},{3,11},{11,3},{4,12},{12,4},... | collective-permute-start | bytes 1843208 | tf_op jit(solution)/shard_map/ppermute | solution.py:480
  190.8 23.1 %collective-permute-start.36 = (bf16[240,1280]{1,0:T(8,128)(2,1)S(1)}, bf16[240,1280]{1,0:T(8,128)(2,1)S(1)}, u32[]{:S(2)}, u32[]{:S(2)}) collective-permute-start(bf16[240,1280]{1,0:T(8,128)(2,1)S(1)} %add.46), channel_id=1, source_target_pairs={{0,4},{2,6},{4,0},{6,2},{1,5},{3,7},{5,1},{7,3},{8,12},{10,14},{12... | collective-permute-start | bytes 1843208 | tf_op jit(solution)/shard_map/ppermute | solution.py:480
  190.8 21.9 %collective-permute-start.33 = (bf16[240,640]{1,0:T(8,128)(2,1)S(1)}, bf16[240,640]{1,0:T(8,128)(2,1)S(1)}, u32[]{:S(2)}, u32[]{:S(2)}) collective-permute-start(bf16[240,640]{1,0:T(8,128)(2,1)S(1)} %bitcast.73), channel_id=1, source_target_pairs={{0,2},{2,0},{4,6},{6,4},{1,3},{3,1},{5,7},{7,5},{8,10},{10,8},{12,... | collective-permute-start | bytes 921608 | tf_op jit(solution)/shard_map/ppermute | solution.py:480
  190.8 21.9 %collective-permute-start.32 = (bf16[16,640]{1,0:T(8,128)(2,1)S(1)}, bf16[16,640]{1,0:T(8,128)(2,1)S(1)}, u32[]{:S(2)}, u32[]{:S(2)}) collective-permute-start(bf16[16,640]{1,0:T(8,128)(2,1)S(1)} %add.47), channel_id=1, source_target_pairs={{0,2},{2,0},{4,6},{6,4},{1,3},{3,1},{5,7},{7,5},{8,10},{10,8},{12,... | collective-permute-start | bytes 61448 | tf_op jit(solution)/shard_map/ppermute | solution.py:480
  214.1 16.0 %collective-permute-start.41 = (bf16[240,1280]{1,0:T(8,128)(2,1)S(1)}, bf16[240,1280]{1,0:T(8,128)(2,1)}, u32[]{:S(2)}, u32[]{:S(2)}) collective-permute-start(bf16[240,1280]{1,0:T(8,128)(2,1)S(1)} %add.49.refs_1_), channel_id=1, source_target_pairs={{0,2},{2,0},{4,6},{6,4},{1,3},{3,1},{5,7},{7,5},{8,10},{10,8},{12,... | collective-permute-start | bytes 1843208 | tf_op jit(solution)/shard_map/ppermute | solution.py:480
  214.9 16.0 %collective-permute-start.42 = (bf16[240,1280]{1,0:T(8,128)(2,1)S(1)}, bf16[240,1280]{1,0:T(8,128)(2,1)S(1)}, u32[]{:S(2)}, u32[]{:S(2)}) collective-permute-start(bf16[240,1280]{1,0:T(8,128)(2,1)S(1)} %add.49.refs_1_), channel_id=1, source_target_pairs={{0,8},{8,0},{1,9},{9,1},{2,10},{10,2},{3,11},{11,3},{4,12},{12,4},... | collective-permute-start | bytes 1843208 | tf_op jit(solution)/shard_map/ppermute | solution.py:480
  230.1 17.0 %collective-permute-start.44 = (bf16[240,1280]{1,0:T(8,128)(2,1)}, bf16[240,1280]{1,0:T(8,128)(2,1)S(1)}, u32[]{:S(2)}, u32[]{:S(2)}) collective-permute-start(bf16[240,1280]{1,0:T(8,128)(2,1)} %collective-permute-done.41.refs_1_), channel_id=1, source_target_pairs={{0,16},{16,0},{1,17},{17,1},{2,18},{18,2},{3,19},{19,3},{4,20},{20... | collective-permute-start | bytes 1843208 | tf_op jit(solution)/shard_map/ppermute | solution.py:480
  230.9 15.4 %collective-permute-start.43 = (bf16[240,640]{1,0:T(8,128)(2,1)S(1)}, bf16[240,640]{1,0:T(8,128)(2,1)S(1)}, u32[]{:S(2)}, u32[]{:S(2)}) collective-permute-start(bf16[240,640]{1,0:T(8,128)(2,1)S(1)} %add.48), channel_id=1, source_target_pairs={{0,4},{2,6},{4,0},{6,2},{1,5},{3,7},{5,1},{7,3},{8,12},{10,14},{12... | collective-permute-start | bytes 921608 | tf_op jit(solution)/shard_map/ppermute | solution.py:480
  235.3 50.0 %collective-permute-start.48 = (bf16[2,240,1280]{2,1,0:T(8,128)(2,1)S(1)}, bf16[2,240,1280]{2,1,0:T(8,128)(2,1)}, u32[]{:S(2)}, u32[]{:S(2)}) collective-permute-start(bf16[2,240,1280]{2,1,0:T(8,128)(2,1)S(1)} %shard_map.256.refs_3_), channel_id=1, source_target_pairs={{0,16},{16,0},{1,17},{17,1},{2,18},{18,2},{3,19},{19,3},{4,20},{20... | collective-permute-start | bytes 3686408 | tf_op jit(solution)/shard_map/ppermute | solution.py:480
  248.8 37.8 %collective-permute-start.50 = (bf16[2,240,1280]{2,1,0:T(8,128)(2,1)S(1)}, bf16[2,240,1280]{2,1,0:T(8,128)(2,1)}, u32[]{:S(2)}, u32[]{:S(2)}) collective-permute-start(bf16[2,240,1280]{2,1,0:T(8,128)(2,1)S(1)} %shard_map.257.refs_3_.refs_5_), channel_id=1, source_target_pairs={{0,8},{8,0},{1,9},{9,1},{2,10},{10,2},{3,11},{11,3},{4,12},{12,4},... | collective-permute-start | bytes 3686408 | tf_op jit(solution)/shard_map/ppermute | solution.py:480
  249.7 9.3 %collective-permute-start.45 = (bf16[240,640]{1,0:T(8,128)(2,1)S(1)}, bf16[240,640]{1,0:T(8,128)(2,1)S(1)}, u32[]{:S(2)}, u32[]{:S(2)}) collective-permute-start(bf16[240,640]{1,0:T(8,128)(2,1)S(1)} %add.50.refs_1_), channel_id=1, source_target_pairs={{0,2},{2,0},{4,6},{6,4},{1,3},{3,1},{5,7},{7,5},{8,10},{10,8},{12,... | collective-permute-start | bytes 921608 | tf_op jit(solution)/shard_map/ppermute | solution.py:480
  250.0 37.9 %collective-permute-start.51 = (bf16[2,240,1280]{2,1,0:T(8,128)(2,1)S(1)}, bf16[2,240,1280]{2,1,0:T(8,128)(2,1)}, u32[]{:S(2)}, u32[]{:S(2)}) collective-permute-start(bf16[2,240,1280]{2,1,0:T(8,128)(2,1)S(1)} %shard_map.256.refs_3_), channel_id=1, source_target_pairs={{0,1},{1,0},{2,3},{3,2},{4,5},{5,4},{6,7},{7,6},{8,9},{9,8},{10,11... | collective-permute-start | bytes 3686408 | tf_op jit(solution)/shard_map/ppermute | solution.py:480
  250.0 9.5 %collective-permute-start.46 = (bf16[16,640]{1,0:T(8,128)(2,1)S(1)}, bf16[16,640]{1,0:T(8,128)(2,1)S(1)}, u32[]{:S(2)}, u32[]{:S(2)}) collective-permute-start(bf16[16,640]{1,0:T(8,128)(2,1)S(1)} %add.51), channel_id=1, source_target_pairs={{0,4},{2,6},{4,0},{6,2},{1,5},{3,7},{5,1},{7,3},{8,12},{10,14},{12... | collective-permute-start | bytes 61448 | tf_op jit(solution)/shard_map/ppermute | solution.py:480
  259.0 24.8 %collective-permute-start.47 = (bf16[240,640]{1,0:T(8,128)(2,1)S(1)}, bf16[240,640]{1,0:T(8,128)(2,1)}, u32[]{:S(2)}, u32[]{:S(2)}) collective-permute-start(bf16[240,640]{1,0:T(8,128)(2,1)S(1)} %add.50.refs_1_), channel_id=1, source_target_pairs={{0,8},{8,0},{1,9},{9,1},{2,10},{10,2},{3,11},{11,3},{4,12},{12,4},... | collective-permute-start | bytes 921608 | tf_op jit(solution)/shard_map/ppermute | solution.py:480
  259.5 25.8 %collective-permute-start.49 = (bf16[240,640]{1,0:T(8,128)(2,1)S(1)}, bf16[240,640]{1,0:T(8,128)(2,1)S(1)}, u32[]{:S(2)}, u32[]{:S(2)}) collective-permute-start(bf16[240,640]{1,0:T(8,128)(2,1)S(1)} %collective-permute-done.45.refs_1_), channel_id=1, source_target_pairs={{0,16},{16,0},{1,17},{17,1},{2,18},{18,2},{3,19},{19,3},{4,20},{20... | collective-permute-start | bytes 921608 | tf_op jit(solution)/shard_map/ppermute | solution.py:480
  286.6 16.3 %collective-permute-start.55 = (bf16[2,240,640]{2,1,0:T(8,128)(2,1)S(1)}, bf16[2,240,640]{2,1,0:T(8,128)(2,1)S(1)}, u32[]{:S(2)}, u32[]{:S(2)}) collective-permute-start(bf16[2,240,640]{2,1,0:T(8,128)(2,1)S(1)} %shard_map.258.refs_3_.refs_1_), channel_id=1, source_target_pairs={{0,16},{16,0},{1,17},{17,1},{2,18},{18,2},{3,19},{19,3},{4,20},{20... | collective-permute-start | bytes 1843208 | tf_op jit(solution)/shard_map/ppermute | solution.py:480
  287.9 15.9 %collective-permute-start.56 = (bf16[2,240,640]{2,1,0:T(8,128)(2,1)S(1)}, bf16[2,240,640]{2,1,0:T(8,128)(2,1)S(1)}, u32[]{:S(2)}, u32[]{:S(2)}) collective-permute-start(bf16[2,240,640]{2,1,0:T(8,128)(2,1)S(1)} %shard_map.259.refs_11_.refs_3_), channel_id=1, source_target_pairs={{0,8},{8,0},{1,9},{9,1},{2,10},{10,2},{3,11},{11,3},{4,12},{12,4},... | collective-permute-start | bytes 1843208 | tf_op jit(solution)/shard_map/ppermute | solution.py:480
  288.7 16.2 %collective-permute-start.57 = (bf16[2,240,640]{2,1,0:T(8,128)(2,1)S(1)}, bf16[2,240,640]{2,1,0:T(8,128)(2,1)S(1)}, u32[]{:S(2)}, u32[]{:S(2)}) collective-permute-start(bf16[2,240,640]{2,1,0:T(8,128)(2,1)S(1)} %shard_map.258.refs_3_.refs_1_), channel_id=1, source_target_pairs={{0,1},{1,0},{2,3},{3,2},{4,5},{5,4},{6,7},{7,6},{8,9},{9,8},{10,11... | collective-permute-start | bytes 1843208 | tf_op jit(solution)/shard_map/ppermute | solution.py:480
  288.7 16.2 %collective-permute-start.59 = (bf16[2,240,640]{2,1,0:T(8,128)(2,1)S(1)}, bf16[2,240,640]{2,1,0:T(8,128)(2,1)S(1)}, u32[]{:S(2)}, u32[]{:S(2)}) collective-permute-start(bf16[2,240,640]{2,1,0:T(8,128)(2,1)S(1)} %shard_map.259.refs_11_.refs_3_), channel_id=1, source_target_pairs={{0,1},{1,0},{2,3},{3,2},{4,5},{5,4},{6,7},{7,6},{8,9},{9,8},{10,11... | collective-permute-start | bytes 1843208 | tf_op jit(solution)/shard_map/ppermute | solution.py:480
  (62 other events, 496.3 us)
